TPU v7x, 32 devices: a whole 2x2x4 slice. The times are simulated.
32 devices in a mesh: groups: 1, node: 32 (over z, y, x, core).
Axes of the slice: x: 2, y: 2, z: 4, core: 2. Of those that a mesh axis runs over, the one named last changes fastest.
Arguments:
- hidden_states: bfloat16 [4096, 4096], P(('groups', 'node'))
- norm_gain: float32 [4096], replicated, may hold values from 0.5 to 1.5
- expert_ids: int32 [4096, 2], P(('groups', 'node')), may hold values from 0 to 15, all different within a row; in each aligned block of 128 rows (0 to 127, 128 to 255, ...) at most 24 rows name the same one
- gate_weights: float32 [4096, 2], P(('groups', 'node')), may hold values from 0.1 to 0.6
- w_gate: bfloat16 [32, 4096, 384], P('node'), may hold values from -0.09375 to 0.09375
- w_up: bfloat16 [32, 4096, 384], P('node'), may hold values from -0.09375 to 0.09375
- w_down: bfloat16 [32, 384, 4096], P('node'), may hold values from -0.21875 to 0.21875
- kv_pages: bfloat16 [256, 16, 1024], P(('groups', 'node')), may hold values from -6 to 6
- page_table: int32 [256, 2], P(('groups', 'node')), may hold values from 0 to 31, as said below
- kv_lengths: int32 [32], P(('groups', 'node')), may hold values from 1 to 8, 160 in all
Outputs:
- moe_output: bfloat16 [4096, 4096], P(('groups', 'node'))
- decode_pages: bfloat16 [256, 16, 1024], P(('groups', 'node'))
Inputs may be any that keep to these rules, and one draw needn't show every extreme that they name: `expert_ids`: each row names 2 different experts. Among the rows of one device no expert is named more than 24 times, and in every draw some expert is named exactly 24 times by the rows of some device. `page_table`: column 0 is a decode device, column 1 a slot below 8. Pages 2i and 2i+1 of a device go to the same decode device; pages of one device with different i go to different decode devices; for each i, different devices send their pages 2i and 2i+1 to different decode devices; no decode slot is named by two pages. The live pages of device s are its first kv_lengths[s] pages.
All inputs are finite; a program needn't handle non-finite values.
Results may differ from a plain program's by a relative error of at most 0.0077.
Values may be sent and summed in bfloat16 or wider, within the bound.
A program may use at most 128 MiB of HBM per device.

v0:
```python
import jax
import jax.numpy as jnp
from jax import lax
from jax.sharding import PartitionSpec as P


def shards(
    hidden_states,
    norm_gain,
    expert_ids,
    gate_weights,
    w_gate,
    w_up,
    w_down,
    kv_pages,
    page_table,
    kv_lengths,
):
    node_count = lax.axis_size("node")
    experts = node_count // 2
    tok_rows, model_width = hidden_states.shape
    top_count = expert_ids.shape[1]
    capacity = tok_rows * top_count * 3 // (2 * experts)
    pages_dev, page_len, kv_width = kv_pages.shape
    is_live = jnp.arange(pages_dev, dtype=jnp.int32) < kv_lengths[0]
    destination = page_table[:, 0]
    slot_index = page_table[:, 1]
    row_target = destination * 2 + jnp.arange(pages_dev, dtype=jnp.int32) % 2
    targets = jnp.arange(node_count * 2, dtype=jnp.int32)
    selector = (targets[:, None] == row_target[None, :]) & is_live[None, :]
    page_rows = jnp.dot(
        selector.astype(jnp.bfloat16),
        kv_pages.reshape(pages_dev, page_len * kv_width),
        preferred_element_type=jnp.float32,
    )
    page_rows = page_rows.astype(jnp.bfloat16).reshape(node_count, 2, page_len * kv_width)
    labels = jnp.sum(jnp.where(selector, slot_index[None, :] + 1, 0), axis=1).reshape(node_count, 2)
    arrived, arrived_labels = (
        lax.all_to_all(page_rows, "node", split_axis=0, concat_axis=0, tiled=True),
        lax.all_to_all(labels, "node", split_axis=0, concat_axis=0, tiled=True),
    )
    placing = (
        arrived_labels.reshape(1, node_count * 2) - 1
        == jnp.arange(pages_dev, dtype=jnp.int32)[:, None]
    )
    decode_pages = jnp.dot(
        placing.astype(jnp.bfloat16),
        arrived.reshape(node_count * 2, page_len * kv_width),
        preferred_element_type=jnp.float32,
    )
    decode_pages = decode_pages.astype(jnp.bfloat16).reshape(pages_dev, page_len, kv_width)
    values = hidden_states.astype(jnp.float32)
    factor = lax.rsqrt(jnp.mean(values * values, axis=1, keepdims=True) + 1e-06)
    normed = (values * factor * norm_gain[None, :]).astype(jnp.bfloat16)
    flat_ids = expert_ids.reshape(-1)
    onehot = (flat_ids[:, None] == jnp.arange(experts, dtype=jnp.int32)[None, :]).astype(jnp.int32)
    before = jnp.cumsum(onehot, axis=0) - onehot
    rank_index = jnp.sum(before * onehot, axis=1)
    slot_of = (flat_ids * capacity + rank_index).reshape(tok_rows, top_count)
    places = jnp.arange(experts * capacity, dtype=jnp.int32)
    placed = jnp.sum(
        (slot_of[None, :, :] == places[:, None, None]).astype(jnp.int32), axis=2
    ).astype(jnp.bfloat16)
    packed = jnp.dot(placed, normed, preferred_element_type=jnp.float32).astype(jnp.bfloat16)
    outgoing = jnp.broadcast_to(
        packed.reshape(experts, 1, capacity, model_width), (experts, 2, capacity, model_width)
    ).reshape(node_count, capacity, model_width)
    gate_local = w_gate[0]
    up_local = w_up[0]
    down_local = w_down[0]
    row_block = lax.all_to_all(outgoing, "node", split_axis=0, concat_axis=0, tiled=True)
    row_count = row_block.shape[1]
    flattened = row_block.reshape(node_count * row_count, row_block.shape[2])
    gate_sum = jnp.dot(flattened, gate_local, preferred_element_type=jnp.float32)
    up_sum = jnp.dot(flattened, up_local, preferred_element_type=jnp.float32)
    activated = (jax.nn.silu(gate_sum) * up_sum).astype(jnp.bfloat16)
    rounded = jnp.dot(activated, down_local, preferred_element_type=jnp.float32).astype(
        jnp.bfloat16
    )
    returned = lax.all_to_all(
        rounded.reshape(node_count, row_count, model_width),
        "node",
        split_axis=0,
        concat_axis=0,
        tiled=True,
    )
    paired = returned.reshape(experts, 2, capacity, model_width)
    expert_out = (paired[:, 0].astype(jnp.float32) + paired[:, 1].astype(jnp.float32)).astype(
        jnp.bfloat16
    )
    picked = jnp.take(expert_out.reshape(experts * capacity, model_width), slot_of, axis=0)
    moe_output = jnp.sum(gate_weights[:, :, None] * picked.astype(jnp.float32), axis=1).astype(
        jnp.bfloat16
    )
    return (moe_output, decode_pages)


def solution(mesh):
    placed = (
        P(("groups", "node"), None),
        P(),
        P(("groups", "node"), None),
        P(("groups", "node"), None),
        P("node", None, None),
        P("node", None, None),
        P("node", None, None),
        P(("groups", "node"), None, None),
        P(("groups", "node"), None),
        P(("groups", "node")),
    )
    return jax.shard_map(
        shards,
        mesh=mesh,
        in_specs=placed,
        out_specs=(P(("groups", "node"), None), P(("groups", "node"), None, None)),
        check_vma=False,
    )
```

profile of v0, /device:TPU:0, one launch (start us, length us, event | category | flops | bytes accessed | tf_op | source)
XLA Modules:
  0.0 396.8 jit_solution(9962836749292692086)
XLA Ops:
  0.6 0.0 copy-start
  0.6 0.8 fusion.27
  1.5 0.8 add_bitcast_fusion.1
  2.9 0.1 select_reduce_fusion
  3.0 0.7 all_to_all.17
  3.7 7.3 %all-to-all-start.2 = ((s32[32,1,2]{2,1,0:T(1,128)}), s32[32,1,2]{2,1,0:T(1,128)S(1)}, u32[]{:S(2)}, u32[]{:S(2)}) async-start(s32[32,1,2]{2,1,0:T(1,128)} %bitcast.13), calls=%async_computation.2 | async-start | bytes 32768 | tf_op jit(solution)/shard_map/all_to_all | solution.py:40
  11.1 0.8 copy.49
  11.8 0.1 eq.70
  12.0 0.1 eq.66
  12.1 0.6 reduce-window.6
  12.7 0.2 slice_reduce_fusion
  13.0 0.1 fusion.20
  13.0 0.1 reduce_sum.48
  13.2 0.1 copy.52
  13.3 0.7 compare_and_fusion
  14.0 1.5 fusion.5
  15.5 4.0 %convolution_convert_fusion.3 = bf16[384,4096]{1,0:T(8,128)(2,1)} fusion(bf16[128,4096]{1,0:T(8,128)(2,1)} %param.10, f32[4096]{0:T(1024)} %param.11, f32[128]{0:T(128)S(1)} %add_rsqrt_fusion, s32[384,128]{1,0:T(8,128)S(1)} %convert_reduce_fusion), kind=kOutput, calls=%fused_computation.5 | convolution fusion | flops 406372352 | bytes 4407808 | tf_op jit(solution)/shard_map/dot_general | solution.py:64
  19.5 0.0 all-to-all-done.2
  19.5 5.3 %broadcast_in_dim.42 = bf16[16,2,24,4096]{3,2,1,0:T(8,128)(2,1)} broadcast(bf16[16,24,4096]{2,1,0:T(8,128)(2,1)} %bitcast.63), dimensions={0,2,3} | broadcast | bytes 9437184 | tf_op jit(solution)/shard_map/broadcast_in_dim | solution.py:65
  24.9 0.0 copy-start.1
  24.9 5.9 %all-to-all-start = ((bf16[32,24,4096]{2,1,0:T(8,128)(2,1)}), bf16[32,24,4096]{2,1,0:T(8,128)(2,1)}, u32[]{:S(2)}, u32[]{:S(2)}) async-start(bf16[32,24,4096]{2,1,0:T(8,128)(2,1)} %bitcast.62), calls=%async_computation | async-start | bytes 12582912 | tf_op jit(solution)/shard_map/all_to_all | solution.py:71
  30.8 0.0 copy-done.1
  30.8 0.2 copy.62
  31.0 2.2 convolution_convert_fusion
  33.2 4.4 %reshape.129 = bf16[32,2,16384]{2,1,0:T(2,128)(2,1)} reshape(bf16[64,16384]{1,0:T(8,128)(2,1)} %convolution_convert_fusion) | data formatting | bytes 4194304 | tf_op jit(solution)/shard_map/reshape | solution.py:36
  37.6 133.3 %all-to-all-done = bf16[32,24,4096]{2,1,0:T(8,128)(2,1)} async-done(((bf16[32,24,4096]{2,1,0:T(8,128)(2,1)}), bf16[32,24,4096]{2,1,0:T(8,128)(2,1)}, u32[]{:S(2)}, u32[]{:S(2)}) %all-to-all-start) | async-done | bytes 6291488 | tf_op jit(solution)/shard_map/all_to_all | solution.py:71
  170.8 3.5 all-to-all-start.3
  174.3 0.0 copy-start.3
  174.3 6.6 %fusion.3 = f32[768,384]{1,0:T(8,128)S(1)} fusion(bf16[768,4096]{1,0:T(8,128)(2,1)} %bitcast.3, bf16[1,4096,384]{2,1,0:T(8,128)(2,1)} %param.14), kind=kOutput, calls=%fused_computation.13 | convolution fusion | flops 2415919104 | bytes 10616832 | tf_op jit(solution)/shard_map/dot_general | solution.py:74
  180.9 0.0 copy-done.3
  180.9 6.3 %fusion.11 = bf16[768,384]{1,0:T(8,128)(2,1)S(1)} fusion(bf16[768,4096]{1,0:T(8,128)(2,1)} %bitcast.3, bf16[1,4096,384]{2,1,0:T(8,128)(2,1)S(1)} %copy-done.3, f32[768,384]{1,0:T(8,128)S(1)} %fusion.3), kind=kOutput, calls=%fused_computation.21 | convolution fusion | flops 2417688576 | bytes 11206656 | tf_op jit(solution)/shard_map/dot_general | solution.py:75
  187.2 0.0 copy-done
  187.2 5.4 %convolution_convert_fusion.2 = bf16[768,4096]{1,0:T(8,128)(2,1)} fusion(bf16[768,384]{1,0:T(8,128)(2,1)S(1)} %fusion.11, bf16[1,384,4096]{2,1,0:T(8,128)(2,1)S(1)} %copy-done), kind=kOutput, calls=%fused_computation.3 | convolution fusion | flops 2419064832 | bytes 10027008 | tf_op jit(solution)/shard_map/dot_general | solution.py:77
  192.7 30.6 %all-to-all-done.3 = bf16[32,2,16384]{2,1,0:T(2,128)(2,1)} async-done(((bf16[32,2,16384]{2,1,0:T(2,128)(2,1)}), bf16[32,2,16384]{2,1,0:T(2,128)(2,1)}, u32[]{:S(2)}, u32[]{:S(2)}) %all-to-all-start.3) | async-done | bytes 2097184 | tf_op jit(solution)/shard_map/all_to_all | solution.py:39
  223.2 0.0 copy-start.2
  223.2 4.2 %all-to-all-start.1 = ((bf16[32,24,4096]{2,1,0:T(8,128)(2,1)}), bf16[32,24,4096]{2,1,0:T(8,128)(2,1)}, u32[]{:S(2)}, u32[]{:S(2)}) async-start(bf16[32,24,4096]{2,1,0:T(8,128)(2,1)} %bitcast.64), calls=%async_computation.1 | async-start | bytes 12582912 | tf_op jit(solution)/shard_map/all_to_all | solution.py:80
  227.4 0.1 copy.56
  227.5 0.1 reshape.134
  227.7 0.1 copy.53
  227.8 0.0 copy-done.2
  227.8 0.1 copy.48
  228.0 0.1 sub.11
  228.1 4.1 %reshape.130 = bf16[64,16384]{1,0:T(8,128)(2,1)} reshape(bf16[32,2,16384]{2,1,0:T(2,128)(2,1)} %all-to-all-done.3) | data formatting | bytes 4194304 | tf_op jit(solution)/shard_map/reshape | solution.py:48
  232.2 2.0 convolution_convert_fusion.1
  234.2 0.9 copy.58
  235.1 132.2 %all-to-all-done.1 = bf16[32,24,4096]{2,1,0:T(8,128)(2,1)} async-done(((bf16[32,24,4096]{2,1,0:T(8,128)(2,1)}), bf16[32,24,4096]{2,1,0:T(8,128)(2,1)}, u32[]{:S(2)}, u32[]{:S(2)}) %all-to-all-start.1) | async-done | bytes 6291488 | tf_op jit(solution)/shard_map/all_to_all | solution.py:80
  367.3 5.9 %add_convert_fusion = bf16[16,1,24,4096]{3,2,0,1:T(8,128)(2,1)} fusion(bf16[16,2,24,4096]{3,2,1,0:T(8,128)(2,1)} %bitcast.8), kind=kLoop, calls=%fused_computation.4 | loop fusion | flops 6291456 | bytes 9437184 | tf_op jit(solution)/shard_map/convert_element_type | solution.py:88
  373.2 7.5 %gather_fusion = bf16[256,4096]{1,0:T(8,128)(2,1)} fusion(bf16[384,4096]{1,0:T(8,128)(2,1)} %bitcast.61, s32[1024]{0:T(1024)S(1)} %pad_clamp_fusion), kind=kCustom, calls=%fused_computation | custom fusion | bytes 4195328 | tf_op jit(solution)/shard_map/jit(_take)/gather | solution.py:91
  380.7 4.4 %reshape.133 = bf16[128,2,4096]{2,1,0:T(2,128)(2,1)} reshape(bf16[256,4096]{1,0:T(8,128)(2,1)} %gather_fusion) | data formatting | bytes 4194304 | tf_op jit(solution)/shard_map/jit(_take)/gather | solution.py:91
  385.1 11.7 %multiply_reduce_fusion = bf16[128,4096]{1,0:T(8,128)(2,1)} fusion(bf16[128,2,4096]{2,1,0:T(2,128)(2,1)} %reshape.133, pred[128,2]{1,0:T(8,128)(4,1)S(1)} %copy.53, f32[128,2]{1,0:T(8,128)S(1)} %copy.48), kind=kLoop, calls=%fused_computation.6 | loop fusion | flops 3670016 | bytes 3147008 | tf_op jit(solution)/shard_map/reduce_sum | solution.py:92
  (9 shorter events, 0.2 us)
Async XLA Ops:
  0.6 186.6 %copy-start = (bf16[1,384,4096]{2,1,0:T(8,128)(2,1)S(1)}, bf16[1,384,4096]{2,1,0:T(8,128)(2,1)}, u32[]{:S(2)}) copy-start(bf16[1,384,4096]{2,1,0:T(8,128)(2,1)} %param.16) | copy-start | bytes 9437188
  3.7 15.8 %all-to-all-start.2 = ((s32[32,1,2]{2,1,0:T(1,128)}), s32[32,1,2]{2,1,0:T(1,128)S(1)}, u32[]{:S(2)}, u32[]{:S(2)}) async-start(s32[32,1,2]{2,1,0:T(1,128)} %bitcast.13), calls=%async_computation.2 | async-start | bytes 32768 | tf_op jit(solution)/shard_map/all_to_all | solution.py:40
  24.9 6.0 %copy-start.1 = (bf16[8,16,1024]{2,1,0:T(8,128)(2,1)S(1)}, bf16[8,16,1024]{2,1,0:T(8,128)(2,1)}, u32[]{:S(2)}) copy-start(bf16[8,16,1024]{2,1,0:T(8,128)(2,1)} %param.17) | copy-start | bytes 786436
  24.9 146.0 %all-to-all-start = ((bf16[32,24,4096]{2,1,0:T(8,128)(2,1)}), bf16[32,24,4096]{2,1,0:T(8,128)(2,1)}, u32[]{:S(2)}, u32[]{:S(2)}) async-start(bf16[32,24,4096]{2,1,0:T(8,128)(2,1)} %bitcast.62), calls=%async_computation | async-start | bytes 12582912 | tf_op jit(solution)/shard_map/all_to_all | solution.py:71
  170.8 52.4 %all-to-all-start.3 = ((bf16[32,2,16384]{2,1,0:T(2,128)(2,1)}), bf16[32,2,16384]{2,1,0:T(2,128)(2,1)}, u32[]{:S(2)}, u32[]{:S(2)}) async-start(bf16[32,2,16384]{2,1,0:T(2,128)(2,1)} %reshape.129), calls=%async_computation.3 | async-start | bytes 4194304 | tf_op jit(solution)/shard_map/all_to_all | solution.py:39
  174.3 6.6 %copy-start.3 = (bf16[1,4096,384]{2,1,0:T(8,128)(2,1)S(1)}, bf16[1,4096,384]{2,1,0:T(8,128)(2,1)}, u32[]{:S(2)}) copy-start(bf16[1,4096,384]{2,1,0:T(8,128)(2,1)} %param.15) | copy-start | bytes 9437188
  223.2 4.6 %copy-start.2 = (f32[128,2]{0,1:T(2,128)S(1)}, f32[128,2]{0,1:T(2,128)}, u32[]{:S(2)}) copy-start(f32[128,2]{0,1:T(2,128)} %param.13) | copy-start | bytes 3076
  223.2 144.1 %all-to-all-start.1 = ((bf16[32,24,4096]{2,1,0:T(8,128)(2,1)}), bf16[32,24,4096]{2,1,0:T(8,128)(2,1)}, u32[]{:S(2)}, u32[]{:S(2)}) async-start(bf16[32,24,4096]{2,1,0:T(8,128)(2,1)} %bitcast.64), calls=%async_computation.1 | async-start | bytes 12582912 | tf_op jit(solution)/shard_map/all_to_all | solution.py:80
where the time goes:
time: 398 us; the launch traced here: 397 us
  waiting for transfers between devices  296 us (74%)
  local copies, waits for them, and re-layouts  29.6 us (7%)
  matrix products  26.4 us (7%)
  other arithmetic  22.4 us (6%)
  starting transfers between devices  20.9 us (5%)
    all_to_all x1, waiting for transfers between devices, shards(): lax.all_to_all(outgoing, 'node', split_axis=0, concat_axis=0, tiled=True)  133 us
    all_to_all x1, waiting for transfers between devices, shards(): lax.all_to_all(rounded.reshape(node_count, row_count, model_width), 'node...  132 us
    all_to_all x1, waiting for transfers between devices, shards(): lax.all_to_all(page_rows, 'node', split_axis=0, concat_axis=0, tiled=True)  30.6 us
    gather x2, local copies, waits for them, and re-layouts, shards(): jnp.take(expert_out.reshape(experts * capacity, model_width), slot_of, ax...  11.9 us
    reduce_sum x1, other arithmetic, shards(): jnp.sum(gate_weights[:, :, None] * picked.astype(jnp.float32), axis=1)  11.7 us
  transfers between devices with their start and end apart: 4, of which 3 were waited for; matrix products, arithmetic and copies ran while one was open for 10% of the time, Pallas kernels for 0%

commit v1 on v0

v1 whole, which is shorter than its diff:
```python
import jax
import jax.numpy as jnp
from jax import lax
from jax.sharding import PartitionSpec as P

BF = jnp.bfloat16
F32 = jnp.float32


def dot32(a, b):
    return jnp.dot(a, b, preferred_element_type=F32)


def all_to_all(x):
    return lax.all_to_all(x, "node", split_axis=0, concat_axis=0, tiled=True)


def pages_phase_one(kv_pages, page_table, kv_lengths, nodes):
    pages_dev, page_len, kv_width = kv_pages.shape
    piece = page_len * kv_width // nodes
    live = jnp.arange(pages_dev, dtype=jnp.int32) < kv_lengths[0]
    code = jnp.where(live, page_table[:, 0] * pages_dev + page_table[:, 1], -1)
    codes = lax.all_gather(code, "node", axis=0, tiled=True)
    pieces = kv_pages.reshape(pages_dev, nodes, piece).swapaxes(0, 1)
    return codes, all_to_all(pieces).reshape(nodes * pages_dev, piece)


def pages_phase_two(codes, pieces, nodes, shape):
    pages_dev = shape[0]
    placing = (codes[None, :] == jnp.arange(codes.shape[0], dtype=jnp.int32)[:, None]).astype(BF)
    sent = dot32(placing, pieces).astype(BF).reshape(nodes, pages_dev, -1)
    return all_to_all(sent).swapaxes(0, 1).reshape(shape)


def shards(
    hidden_states,
    norm_gain,
    expert_ids,
    gate_weights,
    w_gate,
    w_up,
    w_down,
    kv_pages,
    page_table,
    kv_lengths,
):
    nodes = lax.axis_size("node")
    experts = nodes // 2
    core = lax.axis_index("node") % 2
    tok_rows, width = hidden_states.shape
    half = width // 2
    top = expert_ids.shape[1]
    cap = tok_rows * top * 3 // (2 * experts)
    rows = nodes * cap

    codes, pieces = pages_phase_one(kv_pages, page_table, kv_lengths, nodes)

    flat = expert_ids.reshape(-1)
    pairs = flat.shape[0]
    onehot = flat[:, None] == jnp.arange(experts, dtype=jnp.int32)[None, :]
    steps = jnp.arange(pairs, dtype=jnp.int32)
    before = dot32((steps[:, None] > steps[None, :]).astype(BF), onehot.astype(BF))
    rank = jnp.sum(jnp.where(onehot, before, 0.0), axis=1).astype(jnp.int32)
    slot = (flat * (2 * cap) + rank).reshape(tok_rows, top)
    places = jnp.arange(rows, dtype=jnp.int32)

    values = hidden_states.astype(F32)
    factor = lax.rsqrt(jnp.mean(values * values, axis=1, keepdims=True) + 1e-06)
    normed = (values * factor * norm_gain[None, :]).astype(BF)

    def hits(shift):
        return slot[:, :, None] + shift == places[None, None, :]

    placed = jnp.concatenate(
        [jnp.any(hits(0), axis=1), jnp.any(hits(cap), axis=1)], axis=0
    ).astype(BF)
    stacked = jnp.concatenate([normed[:, :half], normed[:, half:]], axis=0)
    outgoing = lax.dot_general(
        placed, stacked, (((0,), (0,)), ((), ())), preferred_element_type=F32
    ).astype(BF)
    mine = all_to_all(outgoing.reshape(nodes, cap, half)).reshape(rows, half)

    swap = [(i, i ^ 1) for i in range(nodes)]
    other = lax.ppermute(mine, "node", swap)
    here, there = core * half, (1 - core) * half

    def halves(w, start, axis):
        return lax.dynamic_slice_in_dim(w, start, half, axis)

    gate = dot32(mine, halves(w_gate[0], here, 0)) + dot32(other, halves(w_gate[0], there, 0))
    up = dot32(mine, halves(w_up[0], here, 0)) + dot32(other, halves(w_up[0], there, 0))
    activated = (jax.nn.silu(gate) * up).astype(BF)
    away = dot32(activated, halves(w_down[0], there, 1)).astype(BF)
    arrived = lax.ppermute(away, "node", swap)
    summed = (dot32(activated, halves(w_down[0], here, 1)) + arrived.astype(F32)).astype(BF)
    returned = all_to_all(summed.reshape(nodes, cap, half)).reshape(rows, half)

    def weights(shift):
        return jnp.sum(jnp.where(hits(shift), gate_weights[:, :, None], 0.0), axis=1)

    scale = jnp.concatenate([weights(0), weights(cap)], axis=0)
    high = scale.astype(BF)
    low = (scale - high.astype(F32)).astype(BF)
    mixed = (dot32(high, returned) + dot32(low, returned)).astype(BF)
    moe_output = jnp.concatenate([mixed[:tok_rows], mixed[tok_rows:]], axis=1)
    decode_pages = pages_phase_two(codes, pieces, nodes, kv_pages.shape)
    return (moe_output, decode_pages)


def solution(mesh):
    placed = (
        P(("groups", "node"), None),
        P(),
        P(("groups", "node"), None),
        P(("groups", "node"), None),
        P("node", None, None),
        P("node", None, None),
        P("node", None, None),
        P(("groups", "node"), None, None),
        P(("groups", "node"), None),
        P(("groups", "node")),
    )
    return jax.shard_map(
        shards,
        mesh=mesh,
        in_specs=placed,
        out_specs=(P(("groups", "node"), None), P(("groups", "node"), None, None)),
        check_vma=False,
    )
```

time: 398 us -> 252 us (0.63)
  waiting for transfers between devices: 296 us -> 71.9 us
  blocking collectives: 0 us -> 119 us
  local copies, waits for them, and re-layouts: 29.6 us -> 7.56 us
  other arithmetic: 22.4 us -> 6.11 us
  starting transfers between devices: 20.9 us -> 12.2 us
  matrix products: 26.4 us -> 33 us
    all_to_all x4 -> x3, waiting for transfers between devices: 296 us -> 71.8 us  [all_to_all(): return lax.all_to_all(x, 'node', split_axis=0, concat_axis=0, tiled=True)]
    all_to_all x0 -> x1, blocking collectives: none -> 78.4 us  [all_to_all(): return lax.all_to_all(x, 'node', split_axis=0, concat_axis=0, tiled=True)]
    unnamed x0 -> x1, blocking collectives: none -> 40.6 us
    gather x2 -> x0, local copies, waits for them, and re-layouts: 11.9 us -> none  [shards(): jnp.take(expert_out.reshape(experts * capacity, model_width), slot_of, ax...]
    reduce_sum x4 -> x1, other arithmetic: 11.9 us -> 0.95 us  [weights(): jnp.sum(jnp.where(hits(shift), gate_weights[:, :, None], 0.0), axis=1)]
    all_to_all x4 -> x3, starting transfers between devices: 20.9 us -> 11.7 us  [all_to_all(): return lax.all_to_all(x, 'node', split_axis=0, concat_axis=0, tiled=True)]
    dot_general x6 -> x11, matrix products: 26.4 us -> 33 us  [the longest x10 31.9 us: dot32(): return jnp.dot(a, b, preferred_element_type=F32)]
    reshape x2, local copies, waits for them, and re-layouts: 8.53 us -> 2.78 us  [the longest x1 1.74 us: pages_phase_two(): return all_to_all(sent).swapaxes(0, 1).reshape(shape)]
  transfers between devices with their start and end apart: 4 -> 5, of which waited for: 3 -> 2; matrix products, arithmetic and copies ran while one was open for 10% -> 8% of each run, Pallas kernels for 0% -> 0%
where the time goes in v1:
time: 252 us; the launch traced here: 251 us
  blocking collectives  119 us (47%)
  waiting for transfers between devices  71.9 us (29%)
  matrix products  33 us (13%)
  starting transfers between devices  12.2 us (5%)
  local copies, waits for them, and re-layouts  7.56 us (3%)
  other arithmetic  6.11 us (2%)
    all_to_all x1, blocking collectives, all_to_all(): return lax.all_to_all(x, 'node', split_axis=0, concat_axis=0, tiled=True)  78.4 us
    all_to_all x3, waiting for transfers between devices, all_to_all(): return lax.all_to_all(x, 'node', split_axis=0, concat_axis=0, tiled=True)  71.8 us
    unnamed x1, blocking collectives  40.6 us
    dot_general x10, matrix products, dot32(): return jnp.dot(a, b, preferred_element_type=F32)  31.9 us
    all_to_all x3, starting transfers between devices, all_to_all(): return lax.all_to_all(x, 'node', split_axis=0, concat_axis=0, tiled=True)  11.7 us
  transfers between devices with their start and end apart: 5, of which 2 were waited for; matrix products, arithmetic and copies ran while one was open for 8% of the time, Pallas kernels for 0%

profile of v1, /device:TPU:0, one launch (start us, length us, event | category | flops | bytes accessed | tf_op | source)
XLA Modules:
  0.0 251.3 jit_solution(943133667281326066)
XLA Ops:
  0.6 0.0 copy-start
  0.6 0.9 copy.40
  1.6 0.1 eq.26
  1.7 0.2 fusion.30
  1.9 0.1 convert_element_type.50
  2.1 0.1 copy.41
  2.1 0.7 broadcast_add_fusion
  2.8 1.5 fusion.1
  4.4 1.6 fusion.3
  5.9 0.1 fusion.59
  6.0 0.2 fusion.34
  6.2 1.0 convolution_convert_fusion.1
  7.3 78.4 %all_to_all.20 = bf16[32,24,2048]{2,1,0:T(8,128)(2,1)} all-to-all(bf16[32,24,2048]{2,1,0:T(8,128)(2,1)S(1)} %bitcast.49), channel_id=1, replica_groups=mesh['groups'=1,'node'=32] {'node'}, dimensions={0} | all-to-all | bytes 6291456 | tf_op jit(solution)/shard_map/all_to_all | solution.py:15
  85.6 0.0 collective-permute-start
  85.6 0.0 copy-start.6
  85.6 4.3 %fusion.15 = f32[768,384]{1,0:T(8,128)S(1)} fusion(bf16[768,2048]{1,0:T(8,128)(2,1)} %bitcast.1, bf16[1,4096,384]{2,1,0:T(8,128)(2,1)} %param.14, s32[]{:T(128)S(6)} %select_n.36), kind=kOutput, calls=%fused_computation.19 | convolution fusion | flops 1207959552 | bytes 5898244 | tf_op jit(solution)/shard_map/dot_general | solution.py:11
  89.9 0.0 copy-done.6
  89.9 0.0 copy-start.5
  90.0 3.8 %fusion.11 = f32[768,384]{1,0:T(8,128)S(1)} fusion(bf16[768,2048]{1,0:T(8,128)(2,1)} %bitcast.1, bf16[1,4096,384]{2,1,0:T(8,128)(2,1)S(1)} %copy-done.6, s32[]{:T(128)S(6)} %select_n.36), kind=kOutput, calls=%fused_computation.15 | convolution fusion | flops 1207959552 | bytes 5898244 | tf_op jit(solution)/shard_map/dot_general | solution.py:11
  93.8 0.0 collective-permute-done
  93.8 0.0 copy-done.5
  93.8 3.7 %fusion.23 = f32[768,384]{1,0:T(8,128)S(1)} fusion(f32[768,384]{1,0:T(8,128)S(1)} %fusion.15, bf16[768,2048]{1,0:T(8,128)(2,1)} %collective-permute-done, bf16[1,4096,384]{2,1,0:T(8,128)(2,1)S(1)} %copy-done.5, s32[]{:T(128)S(6)} %select_n.37), kind=kOutput, calls=%fused_computation.27 | convolution fusion | flops 1208254464 | bytes 7077892 | tf_op jit(solution)/shard_map/dot_general | solution.py:11
  97.6 3.9 %multiply_convert_fusion = bf16[768,384]{1,0:T(8,128)(2,1)S(1)} fusion(f32[768,384]{1,0:T(8,128)S(1)} %fusion.23, f32[768,384]{1,0:T(8,128)S(1)} %fusion.11, bf16[768,2048]{1,0:T(8,128)(2,1)} %collective-permute-done, bf16[1,4096,384]{2,1,0:T(8,128)(2,1)S(1)} %copy-done.6, s32[]{:T(128)S(6)} %select_n.37), kind=kOutput, calls=%fused_computation.30 | convolution fusion | flops 1210023936 | bytes 7667716 | tf_op jit(solution)/shard_map/dot_general | solution.py:11
  101.4 0.0 copy-done
  101.4 0.0 copy-start.7
  101.4 0.0 copy-start.4
  101.5 3.5 %convolution_convert_fusion = bf16[768,2048]{1,0:T(8,128)(2,1)} fusion(bf16[768,384]{1,0:T(8,128)(2,1)S(1)} %multiply_convert_fusion, bf16[1,384,4096]{2,1,0:T(8,128)(2,1)S(1)} %copy-done, s32[]{:T(128)S(6)} %select_n.37), kind=kOutput, calls=%fused_computation.1 | convolution fusion | flops 1209532416 | bytes 5308420 | tf_op jit(solution)/shard_map/dot_general | solution.py:11
  105.0 0.0 copy-done.7
  105.0 0.5 collective-permute-start.1
  105.5 1.0 reshape.66
  106.5 0.9 copy.42
  107.4 3.7 %all-to-all-start.2 = ((bf16[32,8,512]{2,1,0:T(8,128)(2,1)}), bf16[32,8,512]{2,1,0:T(8,128)(2,1)S(1)}, u32[]{:S(2)}, u32[]{:S(2)}) async-start(bf16[32,8,512]{2,1,0:T(8,128)(2,1)} %copy.42), calls=%async_computation.2 | async-start | bytes 524288 | tf_op jit(solution)/shard_map/all_to_all | solution.py:15
  111.7 0.0 copy-done.4
  111.7 0.1 fusion.53
  111.8 40.6 %all-reduce = s32[256]{0:T(256)S(1)} all-reduce(s32[256]{0:T(256)S(1)} %fusion.53), channel_id=1, replica_groups=mesh['groups'=1,'node'=32] {'node'}, use_global_device_ids=true, to_apply=%add | all-reduce | flops 256 | bytes 2048
  152.5 0.0 all-to-all-done.2
  152.5 0.9 fusion.29
  153.4 4.5 %all-to-all-start.3 = ((bf16[32,8,512]{2,1,0:T(8,128)(2,1)}), bf16[32,8,512]{2,1,0:T(8,128)(2,1)S(1)}, u32[]{:S(2)}, u32[]{:S(2)}) async-start(bf16[32,8,512]{2,1,0:T(8,128)(2,1)} %fusion.29), calls=%async_computation.3 | async-start | bytes 524288 | tf_op jit(solution)/shard_map/all_to_all | solution.py:15
  158.0 0.0 collective-permute-done.1
  158.0 5.6 %add_convert_fusion = bf16[768,2048]{1,0:T(8,128)(2,1)} fusion(bf16[768,2048]{1,0:T(8,128)(2,1)} %collective-permute-done.1, bf16[768,384]{1,0:T(8,128)(2,1)} %copy-done.7, bf16[1,384,4096]{2,1,0:T(8,128)(2,1)S(1)} %copy-done, s32[]{:T(128)S(6)} %select_n.36), kind=kOutput, calls=%fused_computation | convolution fusion | flops 1212678144 | bytes 8454148 | tf_op jit(solution)/shard_map/dot_general | solution.py:11
  163.6 4.8 %all-to-all-done.3 = bf16[32,8,512]{2,1,0:T(8,128)(2,1)S(1)} async-done(((bf16[32,8,512]{2,1,0:T(8,128)(2,1)}), bf16[32,8,512]{2,1,0:T(8,128)(2,1)S(1)}, u32[]{:S(2)}, u32[]{:S(2)}) %all-to-all-start.3) | async-done | bytes 262176 | tf_op jit(solution)/shard_map/all_to_all | solution.py:15
  168.4 0.0 copy-start.2
  168.4 0.0 copy-start.3
  168.4 0.7 copy-done.2
  169.1 3.5 %all-to-all-start.1 = ((bf16[32,24,2048]{2,1,0:T(8,128)(2,1)}), bf16[32,24,2048]{2,1,0:T(8,128)(2,1)}, u32[]{:S(2)}, u32[]{:S(2)}) async-start(bf16[32,24,2048]{2,1,0:T(8,128)(2,1)} %bitcast.50), calls=%async_computation.1 | async-start | bytes 6291456 | tf_op jit(solution)/shard_map/all_to_all | solution.py:15
  172.6 0.0 copy-done.3
  172.7 1.0 select_reduce_fusion.1
  173.6 1.7 copy.43
  175.4 1.7 reshape.69
  177.1 67.0 %all-to-all-done.1 = bf16[32,24,2048]{2,1,0:T(8,128)(2,1)} async-done(((bf16[32,24,2048]{2,1,0:T(8,128)(2,1)}), bf16[32,24,2048]{2,1,0:T(8,128)(2,1)}, u32[]{:S(2)}, u32[]{:S(2)}) %all-to-all-start.1) | async-done | bytes 3145760 | tf_op jit(solution)/shard_map/all_to_all | solution.py:15
  244.1 0.0 copy-start.1
  244.1 3.0 %fusion.41 = f32[256,2048]{1,0:T(8,128)S(1)} fusion(bf16[768,2048]{1,0:T(8,128)(2,1)} %bitcast.9, f32[128,768]{1,0:T(8,128)} %get-tuple-element.3, f32[128,768]{1,0:T(8,128)S(1)} %get-tuple-element.2), kind=kOutput, calls=%fused_computation.50 | convolution fusion | flops 806289408 | bytes 6029312 | tf_op jit(solution)/shard_map/dot_general | solution.py:11
  247.2 0.0 copy-done.1
  247.2 2.9 %fusion = bf16[256,2048]{1,0:T(8,128)(2,1)S(1)} fusion(f32[256,2048]{1,0:T(8,128)S(1)} %fusion.41, bf16[768,2048]{1,0:T(8,128)(2,1)} %bitcast.9, f32[128,768]{1,0:T(8,128)S(1)} %copy-done.1, f32[128,768]{1,0:T(8,128)S(1)} %get-tuple-element.2), kind=kOutput, calls=%fused_computation.6 | convolution fusion | flops 807141376 | bytes 7077888 | tf_op jit(solution)/shard_map/dot_general | solution.py:11
  250.1 0.1 fusion.58
  250.2 1.1 pad_maximum_fusion
  (3 shorter events, 0.0 us)
Async XLA Ops:
  0.6 100.8 %copy-start = (bf16[1,384,4096]{2,1,0:T(8,128)(2,1)S(1)}, bf16[1,384,4096]{2,1,0:T(8,128)(2,1)}, u32[]{:S(2)}) copy-start(bf16[1,384,4096]{2,1,0:T(8,128)(2,1)} %param.16) | copy-start | bytes 9437188
  85.6 8.2 %collective-permute-start = (bf16[768,2048]{1,0:T(8,128)(2,1)}, bf16[768,2048]{1,0:T(8,128)(2,1)}, u32[]{:S(2)}, u32[]{:S(2)}) collective-permute-start(bf16[768,2048]{1,0:T(8,128)(2,1)} %bitcast.1), channel_id=1, source_target_pairs={{0,1},{1,0},{2,3},{3,2},{4,5},{5,4},{6,7},{7,6},{8,9},{9,8},{10,11... | collective-permute-start | bytes 9437192 | tf_op jit(solution)/shard_map/ppermute | solution.py:84
  85.6 4.3 %copy-start.6 = (bf16[1,4096,384]{2,1,0:T(8,128)(2,1)S(1)}, bf16[1,4096,384]{2,1,0:T(8,128)(2,1)}, u32[]{:S(2)}) copy-start(bf16[1,4096,384]{2,1,0:T(8,128)(2,1)} %param.15) | copy-start | bytes 9437188
  89.9 3.9 %copy-start.5 = (bf16[1,4096,384]{2,1,0:T(8,128)(2,1)S(1)}, bf16[1,4096,384]{2,1,0:T(8,128)(2,1)}, u32[]{:S(2)}) copy-start(bf16[1,4096,384]{2,1,0:T(8,128)(2,1)} %param.14) | copy-start | bytes 9437188
  101.4 3.5 %copy-start.7 = (bf16[768,384]{1,0:T(8,128)(2,1)}, bf16[768,384]{1,0:T(8,128)(2,1)S(1)}, u32[]{:S(2)}) copy-start(bf16[768,384]{1,0:T(8,128)(2,1)S(1)} %multiply_convert_fusion) | copy-start | bytes 1769476
  101.4 10.3 %copy-start.4 = (s32[8,2]{0,1:T(2,128)S(1)}, s32[8,2]{0,1:T(2,128)}, u32[]{:S(2)}) copy-start(s32[8,2]{0,1:T(2,128)} %param.18) | copy-start | bytes 196
  105.0 53.0 %collective-permute-start.1 = (bf16[768,2048]{1,0:T(8,128)(2,1)}, bf16[768,2048]{1,0:T(8,128)(2,1)}, u32[]{:S(2)}, u32[]{:S(2)}) collective-permute-start(bf16[768,2048]{1,0:T(8,128)(2,1)} %convolution_convert_fusion), channel_id=1, source_target_pairs={{0,1},{1,0},{2,3},{3,2},{4,5},{5,4},{6,7},{7,6},{8,9},{9,8},{10,11... | collective-permute-start | bytes 9437192 | tf_op jit(solution)/shard_map/ppermute | solution.py:94
  107.4 45.1 %all-to-all-start.2 = ((bf16[32,8,512]{2,1,0:T(8,128)(2,1)}), bf16[32,8,512]{2,1,0:T(8,128)(2,1)S(1)}, u32[]{:S(2)}, u32[]{:S(2)}) async-start(bf16[32,8,512]{2,1,0:T(8,128)(2,1)} %copy.42), calls=%async_computation.2 | async-start | bytes 524288 | tf_op jit(solution)/shard_map/all_to_all | solution.py:15
  153.4 15.0 %all-to-all-start.3 = ((bf16[32,8,512]{2,1,0:T(8,128)(2,1)}), bf16[32,8,512]{2,1,0:T(8,128)(2,1)S(1)}, u32[]{:S(2)}, u32[]{:S(2)}) async-start(bf16[32,8,512]{2,1,0:T(8,128)(2,1)} %fusion.29), calls=%async_computation.3 | async-start | bytes 524288 | tf_op jit(solution)/shard_map/all_to_all | solution.py:15
  168.4 0.7 copy-start.2
  168.4 4.2 %copy-start.3 = (f32[128,2]{0,1:T(2,128)S(1)}, f32[128,2]{0,1:T(2,128)}, u32[]{:S(2)}) copy-start(f32[128,2]{0,1:T(2,128)} %param.13) | copy-start | bytes 3076
  169.1 75.0 %all-to-all-start.1 = ((bf16[32,24,2048]{2,1,0:T(8,128)(2,1)}), bf16[32,24,2048]{2,1,0:T(8,128)(2,1)}, u32[]{:S(2)}, u32[]{:S(2)}) async-start(bf16[32,24,2048]{2,1,0:T(8,128)(2,1)} %bitcast.50), calls=%async_computation.1 | async-start | bytes 6291456 | tf_op jit(solution)/shard_map/all_to_all | solution.py:15
  244.1 3.0 %copy-start.1 = (f32[128,768]{1,0:T(8,128)S(1)}, f32[128,768]{1,0:T(8,128)}, u32[]{:S(2)}) copy-start(f32[128,768]{1,0:T(8,128)} %get-tuple-element.3) | copy-start | bytes 1179652

commit v2 on v1

v2 whole, which is shorter than its diff:
```python
import jax
import jax.numpy as jnp
from jax import lax
from jax.sharding import PartitionSpec as P

BF = jnp.bfloat16
F32 = jnp.float32


def dot32(a, b):
    return jnp.dot(a, b, preferred_element_type=F32)


def all_to_all(x):
    return lax.all_to_all(x, "node", split_axis=0, concat_axis=0, tiled=True)


def pages_phase_one(kv_pages, page_table, kv_lengths, nodes):
    pages_dev, page_len, kv_width = kv_pages.shape
    piece = page_len * kv_width // nodes
    live = jnp.arange(pages_dev, dtype=jnp.int32) < kv_lengths[0]
    marks = jnp.stack([jnp.where(live, page_table[:, 0], -1), page_table[:, 1]], axis=1).astype(BF)
    tail = jnp.broadcast_to(jnp.pad(marks, ((0, 0), (0, 126)))[None], (nodes, pages_dev, 128))
    pieces = kv_pages.reshape(pages_dev, nodes, piece).swapaxes(0, 1)
    sent = jnp.concatenate([pieces, tail], axis=2)
    return all_to_all(sent).reshape(nodes * pages_dev, piece + 128)


def pages_phase_two(got, nodes, shape):
    pages_dev = shape[0]
    piece = got.shape[1] - 128
    marks = got[:, piece : piece + 2].astype(jnp.int32)
    code = jnp.where(marks[:, 0] < 0, -1, marks[:, 0] * pages_dev + marks[:, 1])
    placing = (code[None, :] == jnp.arange(code.shape[0], dtype=jnp.int32)[:, None]).astype(BF)
    sent = dot32(placing, got[:, :piece]).astype(BF).reshape(nodes, pages_dev, piece)
    return all_to_all(sent)


def shards(
    hidden_states,
    norm_gain,
    expert_ids,
    gate_weights,
    w_gate,
    w_up,
    w_down,
    kv_pages,
    page_table,
    kv_lengths,
):
    nodes = lax.axis_size("node")
    experts = nodes // 2
    core = lax.axis_index("node") % 2
    tok_rows, width = hidden_states.shape
    half = width // 2
    top = expert_ids.shape[1]
    cap = tok_rows * top * 3 // (2 * experts)
    rows = nodes * cap

    page_pieces = pages_phase_one(kv_pages, page_table, kv_lengths, nodes)

    flat = expert_ids.reshape(-1)
    pairs = flat.shape[0]
    onehot = flat[:, None] == jnp.arange(experts, dtype=jnp.int32)[None, :]
    steps = jnp.arange(pairs, dtype=jnp.int32)
    before = dot32((steps[:, None] > steps[None, :]).astype(BF), onehot.astype(BF))
    rank = jnp.sum(jnp.where(onehot, before, 0.0), axis=1).astype(jnp.int32)
    ids = expert_ids[:, :, None]
    rank = rank.reshape(tok_rows, top, 1)
    values = hidden_states.astype(F32)
    factor = lax.rsqrt(jnp.mean(values * values, axis=1, keepdims=True) + 1e-06)
    normed = (values * factor * norm_gain[None, :]).astype(BF)

    stacked = jnp.concatenate([normed[:, :half], normed[:, half:]], axis=0)
    swap = [(i, i ^ 1) for i in range(nodes)]
    here, there = core * half, (1 - core) * half

    def halves(w, start, axis):
        return lax.dynamic_slice_in_dim(w, start, half, axis)

    gate_here, gate_there = halves(w_gate[0], here, 0), halves(w_gate[0], there, 0)
    up_here, up_there = halves(w_up[0], here, 0), halves(w_up[0], there, 0)
    down_here, down_there = halves(w_down[0], here, 1), halves(w_down[0], there, 1)

    def hits(first, count, second):
        inside = (rank >= first) & (rank < first + count)
        slot = jnp.where(inside, (ids * 2 + second) * count + rank - first, -1)
        return slot == jnp.arange(nodes * count, dtype=jnp.int32)[None, None, :]

    def send(first, count):
        placed = jnp.concatenate(
            [jnp.any(hits(first, count, c), axis=1) for c in (0, 1)], axis=0
        ).astype(BF)
        return lax.dot_general(
            placed, stacked, (((0,), (0,)), ((), ())), preferred_element_type=F32
        ).astype(BF).reshape(nodes, count, half)

    def expert(mine):
        other = lax.ppermute(mine, "node", swap)
        gate = dot32(mine, gate_here) + dot32(other, gate_there)
        up = dot32(mine, up_here) + dot32(other, up_there)
        activated = (jax.nn.silu(gate) * up).astype(BF)
        arrived = lax.ppermute(dot32(activated, down_there).astype(BF), "node", swap)
        return (dot32(activated, down_here) + arrived.astype(F32)).astype(BF)

    def combine(first, count, returned):
        scale = jnp.concatenate(
            [
                jnp.sum(jnp.where(hits(first, count, c), gate_weights[:, :, None], 0.0), axis=1)
                for c in (0, 1)
            ],
            axis=0,
        )
        high = scale.astype(BF)
        low = (scale - high.astype(F32)).astype(BF)
        return dot32(high, returned) + dot32(low, returned)

    large = cap * 2 // 3
    small = cap - large
    one = all_to_all(send(0, large)).reshape(nodes * large, half)
    two_out, one = lax.optimization_barrier((send(large, small), one))
    two = all_to_all(two_out).reshape(nodes * small, half)
    one_done = expert(one)
    slots = pages_phase_two(page_pieces, nodes, kv_pages.shape)
    one_done, two = lax.optimization_barrier((one_done, two))
    one_back = all_to_all(one_done.reshape(nodes, large, half)).reshape(nodes * large, half)
    two_done = expert(two)
    two_done, one_back = lax.optimization_barrier((two_done, one_back))
    two_back = all_to_all(two_done.reshape(nodes, small, half)).reshape(nodes * small, half)
    mixed = (combine(0, large, one_back) + combine(large, small, two_back)).astype(BF)
    moe_output = jnp.concatenate([mixed[:tok_rows], mixed[tok_rows:]], axis=1)
    return (moe_output, slots.swapaxes(0, 1).reshape(kv_pages.shape))


def solution(mesh):
    placed = (
        P(("groups", "node"), None),
        P(),
        P(("groups", "node"), None),
        P(("groups", "node"), None),
        P("node", None, None),
        P("node", None, None),
        P("node", None, None),
        P(("groups", "node"), None, None),
        P(("groups", "node"), None),
        P(("groups", "node")),
    )
    return jax.shard_map(
        shards,
        mesh=mesh,
        in_specs=placed,
        out_specs=(P(("groups", "node"), None), P(("groups", "node"), None, None)),
        check_vma=False,
    )
```

time: 252 us -> 215 us (0.85)
  blocking collectives: 119 us -> 0 us
  waiting for transfers between devices: 71.9 us -> 123 us
  starting transfers between devices: 12.2 us -> 26.8 us
  matrix products: 33 us -> 45.9 us
    all_to_all x1 -> x0, blocking collectives: 78.4 us -> none  [all_to_all(): return lax.all_to_all(x, 'node', split_axis=0, concat_axis=0, tiled=True)]
    all_to_all x3 -> x6, waiting for transfers between devices: 71.8 us -> 123 us  [all_to_all(): return lax.all_to_all(x, 'node', split_axis=0, concat_axis=0, tiled=True)]
    unnamed x1 -> x0, blocking collectives: 40.6 us -> none
    all_to_all x3 -> x6, starting transfers between devices: 11.7 us -> 26 us  [all_to_all(): return lax.all_to_all(x, 'node', split_axis=0, concat_axis=0, tiled=True)]
    dot_general x10 -> x18, matrix products: 31.9 us -> 41.2 us  [dot32(): return jnp.dot(a, b, preferred_element_type=F32)]
    dot_general x1 -> x2, matrix products: 1.03 us -> 4.73 us  [send(): lax.dot_general(placed, stacked, (((0,), (0,)), ((), ())), preferred_elem...]
  transfers between devices with their start and end apart: 5 -> 10, of which waited for: 2 -> 6; matrix products, arithmetic and copies ran while one was open for 8% -> 22% of each run, Pallas kernels for 0% -> 0%
where the time goes in v2:
time: 215 us; the launch traced here: 214 us
  waiting for transfers between devices  123 us (57%)
  matrix products  45.9 us (21%)
  starting transfers between devices  26.8 us (12%)
  other arithmetic  8.53 us (4%)
  local copies, waits for them, and re-layouts  8.22 us (4%)
    all_to_all x6, waiting for transfers between devices, all_to_all(): return lax.all_to_all(x, 'node', split_axis=0, concat_axis=0, tiled=True)  123 us
    dot_general x18, matrix products, dot32(): return jnp.dot(a, b, preferred_element_type=F32)  41.2 us
    all_to_all x6, starting transfers between devices, all_to_all(): return lax.all_to_all(x, 'node', split_axis=0, concat_axis=0, tiled=True)  26 us
    dot_general x2, matrix products, send(): lax.dot_general(placed, stacked, (((0,), (0,)), ((), ())), preferred_elem...  4.73 us
  transfers between devices with their start and end apart: 10, of which 6 were waited for; matrix products, arithmetic and copies ran while one was open for 22% of the time, Pallas kernels for 0%

profile of v2, /device:TPU:0, one launch (start us, length us, event | category | flops | bytes accessed | tf_op | source)
XLA Modules:
  0.0 214.4 jit_solution(7445985075887646993)
XLA Ops:
  0.6 0.0 copy-start
  0.6 0.9 copy.85
  1.6 0.1 eq.38
  1.7 0.2 fusion.57
  1.9 0.1 convert_element_type.86
  2.1 0.1 copy.86
  2.1 0.7 add_select_fusion.3
  2.9 1.5 fusion.3
  4.4 1.6 fusion.5
  5.9 0.1 fusion.107
  6.1 0.2 fusion.61
  6.2 2.1 convolution_convert_fusion
  8.3 7.4 %all-to-all-start = ((bf16[32,16,2048]{2,1,0:T(8,128)(2,1)}), bf16[32,16,2048]{2,1,0:T(8,128)(2,1)}, u32[]{:S(2)}, u32[]{:S(2)}) async-start(bf16[32,16,2048]{2,1,0:T(8,128)(2,1)} %bitcast.80), calls=%async_computation | async-start | bytes 4194304 | tf_op jit(solution)/shard_map/all_to_all | solution.py:15
  15.7 0.1 fusion.70
  15.9 2.7 %fusion.2 = bf16[32,8,2048]{2,1,0:T(8,128)(2,1)} fusion(bf16[128,2048]{1,0:T(8,128)(2,1)} %copy-done.6, bf16[128,2048]{1,0:T(8,128)(2,1)} %copy-done.5, pred[128,256]{1,0:T(8,128)(4,1)S(1)} %get-tuple-element.28, pred[128,256]{1,0:T(8,128)(4,1)S(1)} %get-tuple-element.29), kind=kOutput, calls=%fused_computation.11 | convolution fusion | flops 271122432 | bytes 2162688 | tf_op jit(solution)/shard_map/dot_general | solution.py:94
  18.5 46.1 %all-to-all-done = bf16[32,16,2048]{2,1,0:T(8,128)(2,1)} async-done(((bf16[32,16,2048]{2,1,0:T(8,128)(2,1)}), bf16[32,16,2048]{2,1,0:T(8,128)(2,1)}, u32[]{:S(2)}, u32[]{:S(2)}) %all-to-all-start) | async-done | bytes 2097184 | tf_op jit(solution)/shard_map/all_to_all | solution.py:15
  64.6 0.0 collective-permute-start
  64.6 4.3 %all-to-all-start.1 = ((bf16[32,8,2048]{2,1,0:T(8,128)(2,1)}), bf16[32,8,2048]{2,1,0:T(8,128)(2,1)}, u32[]{:S(2)}, u32[]{:S(2)}) async-start(bf16[32,8,2048]{2,1,0:T(8,128)(2,1)} %fusion.2), calls=%async_computation.1 | async-start | bytes 2097152 | tf_op jit(solution)/shard_map/all_to_all | solution.py:15
  68.9 0.0 copy-start.10
  68.9 3.4 %fusion.30 = f32[512,384]{1,0:T(8,128)S(1)} fusion(bf16[512,2048]{1,0:T(8,128)(2,1)} %bitcast.2, bf16[1,4096,384]{2,1,0:T(8,128)(2,1)} %param.14, s32[]{:T(128)S(6)} %select_n.80), kind=kOutput, calls=%fused_computation.36 | convolution fusion | flops 805306368 | bytes 4456452 | tf_op jit(solution)/shard_map/dot_general | solution.py:11
  72.3 0.0 copy-start.2
  72.3 3.0 %fusion.22 = f32[512,384]{1,0:T(8,128)S(1)} fusion(bf16[512,2048]{1,0:T(8,128)(2,1)} %bitcast.2, bf16[1,4096,384]{2,1,0:T(8,128)(2,1)S(1)} %copy-done.10, s32[]{:T(128)S(6)} %select_n.80), kind=kOutput, calls=%fused_computation.28 | convolution fusion | flops 805306368 | bytes 4456452 | tf_op jit(solution)/shard_map/dot_general | solution.py:11
  75.4 2.9 %fusion.44 = f32[512,384]{1,0:T(8,128)S(1)} fusion(f32[512,384]{1,0:T(8,128)S(1)} %fusion.30, bf16[512,2048]{1,0:T(8,128)(2,1)} %collective-permute-done, bf16[1,4096,384]{2,1,0:T(8,128)(2,1)S(1)} %copy-done.2, s32[]{:T(128)S(6)} %select_n.81), kind=kOutput, calls=%fused_computation.50 | convolution fusion | flops 805502976 | bytes 5242884 | tf_op jit(solution)/shard_map/dot_general | solution.py:11
  78.3 2.9 %multiply_convert_fusion = bf16[512,384]{1,0:T(8,128)(2,1)S(1)} fusion(f32[512,384]{1,0:T(8,128)S(1)} %fusion.44, f32[512,384]{1,0:T(8,128)S(1)} %fusion.22, bf16[512,2048]{1,0:T(8,128)(2,1)} %collective-permute-done, bf16[1,4096,384]{2,1,0:T(8,128)(2,1)S(1)} %copy-done.10, s32[]{:T(128)S(6)} %select_n.81), kind=kOutput, calls=%fused_computation.63 | convolution fusion | flops 806682624 | bytes 5636100 | tf_op jit(solution)/shard_map/dot_general | solution.py:11
  81.2 0.0 copy-start.13
  81.3 2.6 %convolution_convert_fusion.1 = bf16[512,2048]{1,0:T(8,128)(2,1)} fusion(bf16[512,384]{1,0:T(8,128)(2,1)S(1)} %multiply_convert_fusion, bf16[1,384,4096]{2,1,0:T(8,128)(2,1)S(1)} %copy-done, s32[]{:T(128)S(6)} %select_n.81), kind=kOutput, calls=%fused_computation.2 | convolution fusion | flops 806354944 | bytes 4063236 | tf_op jit(solution)/shard_map/dot_general | solution.py:11
  83.8 0.2 collective-permute-start.1
  84.0 1.0 reshape.139
  85.8 0.1 copy.97
  85.9 0.8 copy.95
  86.8 8.3 %all-to-all-done.1 = bf16[32,8,2048]{2,1,0:T(8,128)(2,1)} async-done(((bf16[32,8,2048]{2,1,0:T(8,128)(2,1)}), bf16[32,8,2048]{2,1,0:T(8,128)(2,1)}, u32[]{:S(2)}, u32[]{:S(2)}) %all-to-all-start.1) | async-done | bytes 1048608 | tf_op jit(solution)/shard_map/all_to_all | solution.py:15
  95.1 3.6 %all-to-all-start.4 = ((bf16[32,8,640]{2,1,0:T(8,128)(2,1)}), bf16[32,8,640]{2,1,0:T(8,128)(2,1)S(1)}, u32[]{:S(2)}, u32[]{:S(2)}) async-start(bf16[32,8,640]{2,1,0:T(8,128)(2,1)} %copy.95), calls=%async_computation.4 | async-start | bytes 655360 | tf_op jit(solution)/shard_map/all_to_all | solution.py:15
  98.7 4.3 %add_convert_fusion = bf16[512,2048]{1,0:T(8,128)(2,1)} fusion(bf16[512,2048]{1,0:T(8,128)(2,1)} %collective-permute-done.1, bf16[512,384]{1,0:T(8,128)(2,1)} %copy-done.12, bf16[1,384,4096]{2,1,0:T(8,128)(2,1)S(1)} %copy-done, s32[]{:T(128)S(6)} %select_n.80), kind=kOutput, calls=%fused_computation | convolution fusion | flops 808452096 | bytes 6160388 | tf_op jit(solution)/shard_map/dot_general | solution.py:11
  103.0 7.7 %all-to-all-done.4 = bf16[32,8,640]{2,1,0:T(8,128)(2,1)S(1)} async-done(((bf16[32,8,640]{2,1,0:T(8,128)(2,1)}), bf16[32,8,640]{2,1,0:T(8,128)(2,1)S(1)}, u32[]{:S(2)}, u32[]{:S(2)}) %all-to-all-start.4) | async-done | bytes 327712 | tf_op jit(solution)/shard_map/all_to_all | solution.py:15
  110.7 3.7 %all-to-all-start.2 = ((bf16[32,16,2048]{2,1,0:T(8,128)(2,1)}), bf16[32,16,2048]{2,1,0:T(8,128)(2,1)}, u32[]{:S(2)}, u32[]{:S(2)}) async-start(bf16[32,16,2048]{2,1,0:T(8,128)(2,1)} %bitcast.82), calls=%async_computation.2 | async-start | bytes 4194304 | tf_op jit(solution)/shard_map/all_to_all | solution.py:15
  114.4 0.1 collective-permute-start.2
  114.4 0.0 copy-start.3
  114.5 2.6 %fusion.28 = f32[256,384]{1,0:T(8,128)S(1)} fusion(bf16[256,2048]{1,0:T(8,128)(2,1)} %bitcast.9, bf16[1,4096,384]{2,1,0:T(8,128)(2,1)} %param.14, s32[]{:T(128)S(6)} %select_n.80), kind=kOutput, calls=%fused_computation.34 | convolution fusion | flops 402653184 | bytes 3014660 | tf_op jit(solution)/shard_map/dot_general | solution.py:11
  117.0 2.4 %fusion.20 = f32[256,384]{1,0:T(8,128)S(1)} fusion(bf16[256,2048]{1,0:T(8,128)(2,1)} %bitcast.9, bf16[1,4096,384]{2,1,0:T(8,128)(2,1)} %param.15, s32[]{:T(128)S(6)} %select_n.80), kind=kOutput, calls=%fused_computation.26 | convolution fusion | flops 402653184 | bytes 3014660 | tf_op jit(solution)/shard_map/dot_general | solution.py:11
  119.5 0.0 copy-start.11
  119.5 0.7 fusion.50
  120.2 1.1 copy-done.11
  121.4 0.7 multiply_convert_fusion.1
  122.1 1.7 convolution_convert_fusion.2
  123.8 0.5 collective-permute-start.3
  124.3 0.2 fusion.78
  124.5 0.9 fusion.56
  125.5 37.8 %all-to-all-done.2 = bf16[32,16,2048]{2,1,0:T(8,128)(2,1)} async-done(((bf16[32,16,2048]{2,1,0:T(8,128)(2,1)}), bf16[32,16,2048]{2,1,0:T(8,128)(2,1)}, u32[]{:S(2)}, u32[]{:S(2)}) %all-to-all-start.2) | async-done | bytes 2097184 | tf_op jit(solution)/shard_map/all_to_all | solution.py:15
  163.3 3.7 %all-to-all-start.5 = ((bf16[32,8,512]{2,1,0:T(8,128)(2,1)}), bf16[32,8,512]{2,1,0:T(8,128)(2,1)S(1)}, u32[]{:S(2)}, u32[]{:S(2)}) async-start(bf16[32,8,512]{2,1,0:T(8,128)(2,1)} %fusion.56), calls=%async_computation.5 | async-start | bytes 524288 | tf_op jit(solution)/shard_map/all_to_all | solution.py:15
  167.0 3.0 %add_convert_fusion.1 = bf16[256,2048]{1,0:T(8,128)(2,1)} fusion(bf16[256,2048]{1,0:T(8,128)(2,1)} %collective-permute-done.3, bf16[256,384]{1,0:T(8,128)(2,1)} %copy-done.9, bf16[1,384,4096]{2,1,0:T(8,128)(2,1)S(1)} %copy-done, s32[]{:T(128)S(6)} %select_n.80), kind=kOutput, calls=%fused_computation.15 | convolution fusion | flops 404226048 | bytes 3866628 | tf_op jit(solution)/shard_map/dot_general | solution.py:11
  170.0 7.6 %all-to-all-done.5 = bf16[32,8,512]{2,1,0:T(8,128)(2,1)S(1)} async-done(((bf16[32,8,512]{2,1,0:T(8,128)(2,1)}), bf16[32,8,512]{2,1,0:T(8,128)(2,1)S(1)}, u32[]{:S(2)}, u32[]{:S(2)}) %all-to-all-start.5) | async-done | bytes 262176 | tf_op jit(solution)/shard_map/all_to_all | solution.py:15
  177.6 3.4 %all-to-all-start.3 = ((bf16[32,8,2048]{2,1,0:T(8,128)(2,1)}), bf16[32,8,2048]{2,1,0:T(8,128)(2,1)}, u32[]{:S(2)}, u32[]{:S(2)}) async-start(bf16[32,8,2048]{2,1,0:T(8,128)(2,1)} %bitcast.81), calls=%async_computation.3 | async-start | bytes 2097152 | tf_op jit(solution)/shard_map/all_to_all | solution.py:15
  181.0 1.5 select_reduce_fusion.3
  182.5 1.6 select_reduce_fusion.1
  184.1 1.7 copy.96
  185.9 1.7 reshape.142
  187.6 3.7 %fusion.67 = f32[256,2048]{1,0:T(8,128)} fusion(bf16[512,2048]{1,0:T(8,128)(2,1)} %bitcast.11, f32[128,512]{1,0:T(8,128)} %get-tuple-element.15, f32[128,512]{1,0:T(8,128)S(1)} %get-tuple-element.14), kind=kOutput, calls=%fused_computation.78 | convolution fusion | flops 537395200 | bytes 4718592 | tf_op jit(solution)/shard_map/dot_general | solution.py:11
  191.3 15.9 %all-to-all-done.3 = bf16[32,8,2048]{2,1,0:T(8,128)(2,1)} async-done(((bf16[32,8,2048]{2,1,0:T(8,128)(2,1)}), bf16[32,8,2048]{2,1,0:T(8,128)(2,1)}, u32[]{:S(2)}, u32[]{:S(2)}) %all-to-all-start.3) | async-done | bytes 1048608 | tf_op jit(solution)/shard_map/all_to_all | solution.py:15
  207.2 1.8 fusion.59
  209.0 1.8 convolution_add_fusion.1
  210.8 0.1 copy-done.1
  210.9 2.4 %fusion.1 = bf16[256,2048]{1,0:T(8,128)(2,1)S(1)} fusion(f32[256,2048]{1,0:T(8,128)S(1)} %convolution_add_fusion.1, f32[256,2048]{1,0:T(8,128)S(1)} %copy-done.1, bf16[512,2048]{1,0:T(8,128)(2,1)} %bitcast.11, f32[128,512]{1,0:T(8,128)S(1)} %copy-done.4, f32[128,512]{1,0:T(8,128)S(1)} %get-tuple-element.14), kind=kOutput, calls=%fused_computation.8 | convolution fusion | flops 539099136 | bytes 7864320 | tf_op jit(solution)/shard_map/dot_general | solution.py:11
  213.2 0.1 fusion.106
  213.3 1.1 pad_maximum_fusion.1
  (34 shorter events, 0.2 us)
Async XLA Ops:
  0.6 80.6 %copy-start = (bf16[1,384,4096]{2,1,0:T(8,128)(2,1)S(1)}, bf16[1,384,4096]{2,1,0:T(8,128)(2,1)}, u32[]{:S(2)}) copy-start(bf16[1,384,4096]{2,1,0:T(8,128)(2,1)} %param.16) | copy-start | bytes 9437188
  6.0 2.3 %copy-start.5 = (bf16[128,2048]{1,0:T(8,128)(2,1)}, bf16[128,2048]{1,0:T(8,128)(2,1)S(1)}, u32[]{:S(2)}) copy-start(bf16[128,2048]{1,0:T(8,128)(2,1)S(1)} %get-tuple-element.20) | copy-start | bytes 1572868
  6.1 2.2 %copy-start.6 = (bf16[128,2048]{1,0:T(8,128)(2,1)}, bf16[128,2048]{1,0:T(8,128)(2,1)S(1)}, u32[]{:S(2)}) copy-start(bf16[128,2048]{1,0:T(8,128)(2,1)S(1)} %get-tuple-element.21) | copy-start | bytes 1572868
  8.3 56.3 %all-to-all-start = ((bf16[32,16,2048]{2,1,0:T(8,128)(2,1)}), bf16[32,16,2048]{2,1,0:T(8,128)(2,1)}, u32[]{:S(2)}, u32[]{:S(2)}) async-start(bf16[32,16,2048]{2,1,0:T(8,128)(2,1)} %bitcast.80), calls=%async_computation | async-start | bytes 4194304 | tf_op jit(solution)/shard_map/all_to_all | solution.py:15
  64.6 10.8 %collective-permute-start = (bf16[512,2048]{1,0:T(8,128)(2,1)}, bf16[512,2048]{1,0:T(8,128)(2,1)}, u32[]{:S(2)}, u32[]{:S(2)}) collective-permute-start(bf16[512,2048]{1,0:T(8,128)(2,1)} %bitcast.2), channel_id=1, source_target_pairs={{0,1},{1,0},{2,3},{3,2},{4,5},{5,4},{6,7},{7,6},{8,9},{9,8},{10,11... | collective-permute-start | bytes 6291464 | tf_op jit(solution)/shard_map/ppermute | solution.py:99
  64.6 30.5 %all-to-all-start.1 = ((bf16[32,8,2048]{2,1,0:T(8,128)(2,1)}), bf16[32,8,2048]{2,1,0:T(8,128)(2,1)}, u32[]{:S(2)}, u32[]{:S(2)}) async-start(bf16[32,8,2048]{2,1,0:T(8,128)(2,1)} %fusion.2), calls=%async_computation.1 | async-start | bytes 2097152 | tf_op jit(solution)/shard_map/all_to_all | solution.py:15
  68.9 3.5 %copy-start.10 = (bf16[1,4096,384]{2,1,0:T(8,128)(2,1)S(1)}, bf16[1,4096,384]{2,1,0:T(8,128)(2,1)}, u32[]{:S(2)}) copy-start(bf16[1,4096,384]{2,1,0:T(8,128)(2,1)} %param.15) | copy-start | bytes 9437188
  72.3 3.0 %copy-start.2 = (bf16[1,4096,384]{2,1,0:T(8,128)(2,1)S(1)}, bf16[1,4096,384]{2,1,0:T(8,128)(2,1)}, u32[]{:S(2)}) copy-start(bf16[1,4096,384]{2,1,0:T(8,128)(2,1)} %param.14) | copy-start | bytes 9437188
  81.2 2.6 %copy-start.12 = (bf16[512,384]{1,0:T(8,128)(2,1)}, bf16[512,384]{1,0:T(8,128)(2,1)S(1)}, u32[]{:S(2)}) copy-start(bf16[512,384]{1,0:T(8,128)(2,1)S(1)} %multiply_convert_fusion) | copy-start | bytes 1179652
  81.2 4.5 %copy-start.13 = (s32[8,2]{0,1:T(2,128)S(1)}, s32[8,2]{0,1:T(2,128)}, u32[]{:S(2)}) copy-start(s32[8,2]{0,1:T(2,128)} %param.18) | copy-start | bytes 196
  83.8 14.9 %collective-permute-start.1 = (bf16[512,2048]{1,0:T(8,128)(2,1)}, bf16[512,2048]{1,0:T(8,128)(2,1)}, u32[]{:S(2)}, u32[]{:S(2)}) collective-permute-start(bf16[512,2048]{1,0:T(8,128)(2,1)} %convolution_convert_fusion.1), channel_id=1, source_target_pairs={{0,1},{1,0},{2,3},{3,2},{4,5},{5,4},{6,7},{7,6},{8,9},{9,8},{10,11... | collective-permute-start | bytes 6291464 | tf_op jit(solution)/shard_map/ppermute | solution.py:103
  95.1 15.6 %all-to-all-start.4 = ((bf16[32,8,640]{2,1,0:T(8,128)(2,1)}), bf16[32,8,640]{2,1,0:T(8,128)(2,1)S(1)}, u32[]{:S(2)}, u32[]{:S(2)}) async-start(bf16[32,8,640]{2,1,0:T(8,128)(2,1)} %copy.95), calls=%async_computation.4 | async-start | bytes 655360 | tf_op jit(solution)/shard_map/all_to_all | solution.py:15
  110.7 52.6 %all-to-all-start.2 = ((bf16[32,16,2048]{2,1,0:T(8,128)(2,1)}), bf16[32,16,2048]{2,1,0:T(8,128)(2,1)}, u32[]{:S(2)}, u32[]{:S(2)}) async-start(bf16[32,16,2048]{2,1,0:T(8,128)(2,1)} %bitcast.82), calls=%async_computation.2 | async-start | bytes 4194304 | tf_op jit(solution)/shard_map/all_to_all | solution.py:15
  114.4 5.1 %collective-permute-start.2 = (bf16[256,2048]{1,0:T(8,128)(2,1)}, bf16[256,2048]{1,0:T(8,128)(2,1)S(1)}, u32[]{:S(2)}, u32[]{:S(2)}) collective-permute-start(bf16[256,2048]{1,0:T(8,128)(2,1)} %bitcast.9), channel_id=1, source_target_pairs={{0,1},{1,0},{2,3},{3,2},{4,5},{5,4},{6,7},{7,6},{8,9},{9,8},{10,11... | collective-permute-start | bytes 3145736 | tf_op jit(solution)/shard_map/ppermute | solution.py:99
  114.4 5.1 %copy-start.3 = (bf16[1,4096,384]{2,1,0:T(8,128)(2,1)S(1)}, bf16[1,4096,384]{2,1,0:T(8,128)(2,1)}, u32[]{:S(2)}) copy-start(bf16[1,4096,384]{2,1,0:T(8,128)(2,1)} %param.14) | copy-start | bytes 9437188
  119.5 1.9 copy-start.11
  122.1 2.4 %copy-start.9 = (bf16[256,384]{1,0:T(8,128)(2,1)}, bf16[256,384]{1,0:T(8,128)(2,1)S(1)}, u32[]{:S(2)}) copy-start(bf16[256,384]{1,0:T(8,128)(2,1)S(1)} %multiply_convert_fusion.1) | copy-start | bytes 589828
  123.8 43.2 %collective-permute-start.3 = (bf16[256,2048]{1,0:T(8,128)(2,1)}, bf16[256,2048]{1,0:T(8,128)(2,1)}, u32[]{:S(2)}, u32[]{:S(2)}) collective-permute-start(bf16[256,2048]{1,0:T(8,128)(2,1)} %convolution_convert_fusion.2), channel_id=1, source_target_pairs={{0,1},{1,0},{2,3},{3,2},{4,5},{5,4},{6,7},{7,6},{8,9},{9,8},{10,11... | collective-permute-start | bytes 3145736 | tf_op jit(solution)/shard_map/ppermute | solution.py:103
  163.3 14.3 %all-to-all-start.5 = ((bf16[32,8,512]{2,1,0:T(8,128)(2,1)}), bf16[32,8,512]{2,1,0:T(8,128)(2,1)S(1)}, u32[]{:S(2)}, u32[]{:S(2)}) async-start(bf16[32,8,512]{2,1,0:T(8,128)(2,1)} %fusion.56), calls=%async_computation.5 | async-start | bytes 524288 | tf_op jit(solution)/shard_map/all_to_all | solution.py:15
  177.6 3.4 %copy-start.8 = (bf16[32,8,512]{2,1,0:T(8,128)(2,1)}, bf16[32,8,512]{2,1,0:T(8,128)(2,1)S(1)}, u32[]{:S(2)}) copy-start(bf16[32,8,512]{2,1,0:T(8,128)(2,1)S(1)} %all-to-all-done.5) | copy-start | bytes 786436
  177.6 29.6 %all-to-all-start.3 = ((bf16[32,8,2048]{2,1,0:T(8,128)(2,1)}), bf16[32,8,2048]{2,1,0:T(8,128)(2,1)}, u32[]{:S(2)}, u32[]{:S(2)}) async-start(bf16[32,8,2048]{2,1,0:T(8,128)(2,1)} %bitcast.81), calls=%async_computation.3 | async-start | bytes 2097152 | tf_op jit(solution)/shard_map/all_to_all | solution.py:15
  207.2 1.8 copy-start.7
  208.9 1.9 copy-start.1
  209.0 1.9 copy-start.4

commit v3 on v2

v3 whole, which is shorter than its diff:
```python
import jax
import jax.numpy as jnp
from jax import lax
from jax.sharding import PartitionSpec as P

BF = jnp.bfloat16
F32 = jnp.float32


def dot32(a, b):
    return jnp.dot(a, b, preferred_element_type=F32)


def all_to_all(x, groups=None):
    return lax.all_to_all(
        x, "node", split_axis=0, concat_axis=0, axis_index_groups=groups, tiled=True
    )


def pages_phase_one(kv_pages, page_table, kv_lengths, nodes):
    pages_dev, page_len, kv_width = kv_pages.shape
    piece = page_len * kv_width // nodes
    live = jnp.arange(pages_dev, dtype=jnp.int32) < kv_lengths[0]
    marks = jnp.stack([jnp.where(live, page_table[:, 0], -1), page_table[:, 1]], axis=1).astype(BF)
    tail = jnp.broadcast_to(jnp.pad(marks, ((0, 0), (0, 126)))[None], (nodes, pages_dev, 128))
    pieces = kv_pages.reshape(pages_dev, nodes, piece).swapaxes(0, 1)
    sent = jnp.concatenate([pieces, tail], axis=2)
    return all_to_all(sent).reshape(nodes * pages_dev, piece + 128)


def pages_phase_two(got, nodes, shape):
    pages_dev = shape[0]
    piece = got.shape[1] - 128
    marks = got[:, piece : piece + 2].astype(jnp.int32)
    code = jnp.where(marks[:, 0] < 0, -1, marks[:, 0] * pages_dev + marks[:, 1])
    placing = (code[None, :] == jnp.arange(code.shape[0], dtype=jnp.int32)[:, None]).astype(BF)
    sent = dot32(placing, got[:, :piece]).astype(BF).reshape(nodes, pages_dev, piece)
    return all_to_all(sent)


def shards(
    hidden_states,
    norm_gain,
    expert_ids,
    gate_weights,
    w_gate,
    w_up,
    w_down,
    kv_pages,
    page_table,
    kv_lengths,
):
    nodes = lax.axis_size("node")
    experts = nodes // 2
    tok_rows, width = hidden_states.shape
    top = expert_ids.shape[1]
    cap = tok_rows * top * 3 // (2 * experts)

    page_pieces = pages_phase_one(kv_pages, page_table, kv_lengths, nodes)

    flat = expert_ids.reshape(-1)
    pairs = flat.shape[0]
    onehot = flat[:, None] == jnp.arange(experts, dtype=jnp.int32)[None, :]
    steps = jnp.arange(pairs, dtype=jnp.int32)
    before = dot32((steps[:, None] > steps[None, :]).astype(BF), onehot.astype(BF))
    rank = jnp.sum(jnp.where(onehot, before, 0.0), axis=1).astype(jnp.int32)
    ids = expert_ids[:, :, None]
    rank = rank.reshape(tok_rows, top, 1)
    values = hidden_states.astype(F32)
    factor = lax.rsqrt(jnp.mean(values * values, axis=1, keepdims=True) + 1e-06)
    normed = (values * factor * norm_gain[None, :]).astype(BF)

    swap = [(i, i ^ 1) for i in range(nodes)]
    parity = [list(range(c, nodes, 2)) for c in (0, 1)]

    def both(w):
        return w[0], lax.ppermute(w, "node", swap)[0]

    weights = list(zip(both(w_gate), both(w_up), both(w_down)))

    def hits(first, count):
        inside = (rank >= first) & (rank < first + count)
        slot = jnp.where(inside, ids * count + rank - first, -1)
        return slot == jnp.arange(experts * count, dtype=jnp.int32)[None, None, :]

    def send(first, count):
        placed = jnp.any(hits(first, count), axis=1).astype(BF)
        rows = lax.dot_general(
            placed, normed, (((0,), (0,)), ((), ())), preferred_element_type=F32
        )
        return rows.astype(BF).reshape(experts, count, width)

    def exchange(x):
        return all_to_all(x.reshape(experts, -1, width), parity).reshape(-1, width)

    def expert(x):
        total = None
        for gate_w, up_w, down_w in weights:
            activated = (jax.nn.silu(dot32(x, gate_w)) * dot32(x, up_w)).astype(BF)
            part = dot32(activated, down_w)
            total = part if total is None else total + part
        return total.astype(BF)

    def combine(first, count, returned):
        scale = jnp.sum(jnp.where(hits(first, count), gate_weights[:, :, None], 0.0), axis=1)
        high = scale.astype(BF)
        low = (scale - high.astype(F32)).astype(BF)
        return dot32(high, returned) + dot32(low, returned)

    large = cap * 2 // 3
    small = cap - large
    one_out, page_pieces = lax.optimization_barrier((send(0, large), page_pieces))
    one = exchange(one_out)
    two_out, one = lax.optimization_barrier((send(large, small), one))
    two = exchange(two_out)
    one_done = expert(one)
    slots = pages_phase_two(page_pieces, nodes, kv_pages.shape)
    one_done, two = lax.optimization_barrier((one_done, two))
    one_back = exchange(one_done)
    two_done = expert(two)
    two_done, one_back = lax.optimization_barrier((two_done, one_back))
    two_back = exchange(two_done)
    moe_output = (combine(0, large, one_back) + combine(large, small, two_back)).astype(BF)
    return (moe_output, slots.swapaxes(0, 1).reshape(kv_pages.shape))


def solution(mesh):
    placed = (
        P(("groups", "node"), None),
        P(),
        P(("groups", "node"), None),
        P(("groups", "node"), None),
        P("node", None, None),
        P("node", None, None),
        P("node", None, None),
        P(("groups", "node"), None, None),
        P(("groups", "node"), None),
        P(("groups", "node")),
    )
    return jax.shard_map(
        shards,
        mesh=mesh,
        in_specs=placed,
        out_specs=(P(("groups", "node"), None), P(("groups", "node"), None, None)),
        check_vma=False,
    )
```

time: 215 us -> 203 us (0.944)
  waiting for transfers between devices: 123 us -> 103 us
  starting transfers between devices: 26.8 us -> 40.3 us
  other arithmetic: 8.53 us -> 3.02 us
  matrix products: 45.9 us -> 49.4 us
  local copies, waits for them, and re-layouts: 8.22 us -> 5.07 us
    all_to_all x6, waiting for transfers between devices: 123 us -> 103 us  [all_to_all(): lax.all_to_all(x, 'node', split_axis=0, concat_axis=0, axis_index_groups=...]
    all_to_all x6, starting transfers between devices: 26 us -> 39.6 us  [all_to_all(): lax.all_to_all(x, 'node', split_axis=0, concat_axis=0, axis_index_groups=...]
    dot_general x18 -> x14, matrix products: 41.2 us -> 45.8 us  [dot32(): return jnp.dot(a, b, preferred_element_type=F32)]
    reduce_sum x2, other arithmetic: 3.13 us -> 0.89 us  [combine(): jnp.sum(jnp.where(hits(first, count), gate_weights[:, :, None], 0.0), axi...]
  transfers between devices with their start and end apart: 10 -> 9, of which waited for: 6 -> 6; matrix products, arithmetic and copies ran while one was open for 22% -> 26% of each run, Pallas kernels for 0% -> 0%
where the time goes in v3:
time: 203 us; the launch traced here: 202 us
  waiting for transfers between devices  103 us (51%)
  matrix products  49.4 us (24%)
  starting transfers between devices  40.3 us (20%)
  local copies, waits for them, and re-layouts  5.07 us (2%)
  other arithmetic  3.02 us (1%)
    all_to_all x6, waiting for transfers between devices, all_to_all(): lax.all_to_all(x, 'node', split_axis=0, concat_axis=0, axis_index_groups=...  103 us
    dot_general x14, matrix products, dot32(): return jnp.dot(a, b, preferred_element_type=F32)  45.8 us
    all_to_all x6, starting transfers between devices, all_to_all(): lax.all_to_all(x, 'node', split_axis=0, concat_axis=0, axis_index_groups=...  39.6 us
  transfers between devices with their start and end apart: 9, of which 6 were waited for; matrix products, arithmetic and copies ran while one was open for 26% of the time, Pallas kernels for 0%

profile of v3, /device:TPU:0, one launch (start us, length us, event | category | flops | bytes accessed | tf_op | source)
XLA Modules:
  0.0 202.2 jit_solution(6722509863999284155)
XLA Ops:
  0.6 0.0 copy-start.5
  0.6 0.0 copy-start
  0.7 0.0 copy-start.3
  0.7 1.1 reshape.112
  2.4 0.7 convert.8
  3.1 0.7 fusion.87
  3.8 0.1 copy.67
  4.0 0.8 copy.65
  4.8 7.3 %all-to-all-start = ((bf16[32,8,640]{2,1,0:T(8,128)(2,1)}), bf16[32,8,640]{2,1,0:T(8,128)(2,1)S(1)}, u32[]{:S(2)}, u32[]{:S(2)}) async-start(bf16[32,8,640]{2,1,0:T(8,128)(2,1)} %copy.65), calls=%async_computation | async-start | bytes 655360 | tf_op jit(solution)/shard_map/all_to_all | solution.py:15
  12.1 0.0 copy-done.5
  12.1 0.1 copy.57
  12.2 0.1 eq.24
  12.4 0.2 fusion.47
  12.6 0.1 convert_element_type.78
  12.7 0.1 copy.58
  12.8 0.0 copy-done
  12.8 0.3 fusion.27
  13.1 0.1 fusion.59
  13.3 0.0 copy-done.3
  13.3 2.2 %convolution_convert_fusion = bf16[256,4096]{1,0:T(8,128)(2,1)} fusion(pred[128,256]{1,0:T(8,128)(4,1)S(1)} %fusion.59, bf16[128,4096]{1,0:T(8,128)(2,1)S(1)} %copy-done, f32[4096]{0:T(1024)S(1)} %copy-done.3, f32[128]{0:T(128)S(1)} %add_rsqrt_fusion), kind=kOutput, calls=%fused_computation.1 | convolution fusion | flops 271581184 | bytes 3195392 | tf_op jit(solution)/shard_map/dot_general | solution.py:88
  15.4 8.7 %all-to-all-done = bf16[32,8,640]{2,1,0:T(8,128)(2,1)S(1)} async-done(((bf16[32,8,640]{2,1,0:T(8,128)(2,1)}), bf16[32,8,640]{2,1,0:T(8,128)(2,1)S(1)}, u32[]{:S(2)}, u32[]{:S(2)}) %all-to-all-start) | async-done | bytes 327712 | tf_op jit(solution)/shard_map/all_to_all | solution.py:15
  24.1 3.7 %all-to-all-start.1 = ((bf16[16,16,4096]{2,1,0:T(8,128)(2,1)}), bf16[16,16,4096]{2,1,0:T(8,128)(2,1)S(1)}, u32[]{:S(2)}, u32[]{:S(2)}) async-start(bf16[16,16,4096]{2,1,0:T(8,128)(2,1)} %bitcast.93), calls=%async_computation.1 | async-start | bytes 4194304 | tf_op jit(solution)/shard_map/all_to_all | solution.py:15
  27.8 0.1 collective-permute-start.1
  27.9 0.5 collective-permute-start
  28.4 0.1 collective-permute-start.2
  28.5 0.1 fusion.74
  28.6 1.5 fusion.4
  30.1 40.8 %all-to-all-done.1 = bf16[16,16,4096]{2,1,0:T(8,128)(2,1)S(1)} async-done(((bf16[16,16,4096]{2,1,0:T(8,128)(2,1)}), bf16[16,16,4096]{2,1,0:T(8,128)(2,1)S(1)}, u32[]{:S(2)}, u32[]{:S(2)}) %all-to-all-start.1) | async-done | bytes 2097184 | tf_op jit(solution)/shard_map/all_to_all | solution.py:15
  70.9 9.9 %all-to-all-start.2 = ((bf16[16,8,4096]{2,1,0:T(8,128)(2,1)}), bf16[16,8,4096]{2,1,0:T(8,128)(2,1)S(1)}, u32[]{:S(2)}, u32[]{:S(2)}) async-start(bf16[16,8,4096]{2,1,0:T(8,128)(2,1)} %fusion.4), calls=%async_computation.2 | async-start | bytes 2097152 | tf_op jit(solution)/shard_map/all_to_all | solution.py:15
  80.8 3.9 %fusion.25 = f32[256,384]{1,0:T(8,128)} fusion(bf16[256,4096]{1,0:T(8,128)(2,1)S(1)} %bitcast.86, bf16[1,4096,384]{2,1,0:T(8,128)(2,1)} %param.14), kind=kOutput, calls=%fused_computation.31 | convolution fusion | flops 805306368 | bytes 5636096 | tf_op jit(solution)/shard_map/dot_general | solution.py:11
  84.7 0.0 collective-permute-done.1
  84.7 3.9 %fusion.9 = f32[256,384]{1,0:T(8,128)} fusion(bf16[256,4096]{1,0:T(8,128)(2,1)S(1)} %bitcast.87, bf16[1,4096,384]{2,1,0:T(8,128)(2,1)} %collective-permute-done.1), kind=kOutput, calls=%fused_computation.15 | convolution fusion | flops 805306368 | bytes 5636096 | tf_op jit(solution)/shard_map/dot_general | solution.py:11
  88.6 7.4 %fusion.17 = f32[256,4096]{1,0:T(8,128)} fusion(bf16[1,384,4096]{2,1,0:T(8,128)(2,1)} %param.16, bf16[256,4096]{1,0:T(8,128)(2,1)S(1)} %bitcast.88, bf16[1,4096,384]{2,1,0:T(8,128)(2,1)} %param.15, f32[256,384]{1,0:T(8,128)} %fusion.25), kind=kOutput, calls=%fused_computation.23 | convolution fusion | flops 1611202560 | bytes 12976128 | tf_op jit(solution)/shard_map/dot_general | solution.py:11
  96.0 0.0 collective-permute-done
  96.0 0.0 collective-permute-done.2
  96.0 8.0 %fusion = bf16[256,4096]{1,0:T(8,128)(2,1)} fusion(f32[256,4096]{1,0:T(8,128)} %fusion.17, bf16[1,384,4096]{2,1,0:T(8,128)(2,1)} %collective-permute-done.2, f32[256,384]{1,0:T(8,128)} %fusion.9, bf16[256,4096]{1,0:T(8,128)(2,1)S(1)} %bitcast.89, bf16[1,4096,384]{2,1,0:T(8,128)(2,1)} %collective-permute-done), kind=kOutput, calls=%fused_computation.2 | convolution fusion | flops 1613299712 | bytes 15073280 | tf_op jit(solution)/shard_map/dot_general | solution.py:11
  103.9 0.5 all-to-all-done.2
  104.4 6.4 %all-to-all-start.3 = ((bf16[16,16,4096]{2,1,0:T(8,128)(2,1)}), bf16[16,16,4096]{2,1,0:T(8,128)(2,1)S(1)}, u32[]{:S(2)}, u32[]{:S(2)}) async-start(bf16[16,16,4096]{2,1,0:T(8,128)(2,1)} %bitcast.92), calls=%async_computation.3 | async-start | bytes 4194304 | tf_op jit(solution)/shard_map/all_to_all | solution.py:15
  110.9 0.2 fusion.72
  111.1 1.0 fusion.36
  112.0 2.6 %fusion.23 = f32[128,384]{1,0:T(8,128)S(1)} fusion(bf16[128,4096]{1,0:T(8,128)(2,1)S(1)} %bitcast.82, bf16[1,4096,384]{2,1,0:T(8,128)(2,1)} %param.14), kind=kOutput, calls=%fused_computation.29 | convolution fusion | flops 402653184 | bytes 4390912 | tf_op jit(solution)/shard_map/dot_general | solution.py:11
  114.6 3.3 %fusion.7 = f32[128,384]{1,0:T(8,128)} fusion(bf16[128,4096]{1,0:T(8,128)(2,1)S(1)} %bitcast.83, bf16[1,4096,384]{2,1,0:T(8,128)(2,1)} %collective-permute-done.1), kind=kOutput, calls=%fused_computation.13 | convolution fusion | flops 402653184 | bytes 4390912 | tf_op jit(solution)/shard_map/dot_general | solution.py:11
  117.9 5.5 %fusion.15 = f32[128,4096]{1,0:T(8,128)} fusion(bf16[1,384,4096]{2,1,0:T(8,128)(2,1)} %param.16, bf16[128,4096]{1,0:T(8,128)(2,1)S(1)} %bitcast.84, bf16[1,4096,384]{2,1,0:T(8,128)(2,1)} %param.15, f32[128,384]{1,0:T(8,128)S(1)} %fusion.23), kind=kOutput, calls=%fused_computation.21 | convolution fusion | flops 805601280 | bytes 9633792 | tf_op jit(solution)/shard_map/dot_general | solution.py:11
  123.4 29.4 %all-to-all-done.3 = bf16[16,16,4096]{2,1,0:T(8,128)(2,1)S(1)} async-done(((bf16[16,16,4096]{2,1,0:T(8,128)(2,1)}), bf16[16,16,4096]{2,1,0:T(8,128)(2,1)S(1)}, u32[]{:S(2)}, u32[]{:S(2)}) %all-to-all-start.3) | async-done | bytes 2097184 | tf_op jit(solution)/shard_map/all_to_all | solution.py:15
  152.8 8.7 %all-to-all-start.5 = ((bf16[32,8,512]{2,1,0:T(8,128)(2,1)}), bf16[32,8,512]{2,1,0:T(8,128)(2,1)S(1)}, u32[]{:S(2)}, u32[]{:S(2)}) async-start(bf16[32,8,512]{2,1,0:T(8,128)(2,1)} %fusion.36), calls=%async_computation.5 | async-start | bytes 524288 | tf_op jit(solution)/shard_map/all_to_all | solution.py:15
  161.5 5.9 %fusion.2 = bf16[128,4096]{1,0:T(8,128)(2,1)} fusion(f32[128,4096]{1,0:T(8,128)} %fusion.15, bf16[1,384,4096]{2,1,0:T(8,128)(2,1)} %collective-permute-done.2, f32[128,384]{1,0:T(8,128)} %fusion.7, bf16[128,4096]{1,0:T(8,128)(2,1)S(1)} %bitcast.85, bf16[1,4096,384]{2,1,0:T(8,128)(2,1)} %collective-permute-done), kind=kOutput, calls=%fused_computation.7 | convolution fusion | flops 806649856 | bytes 10682368 | tf_op jit(solution)/shard_map/dot_general | solution.py:11
  167.4 0.0 copy-start.4
  167.4 4.7 %all-to-all-done.5 = bf16[32,8,512]{2,1,0:T(8,128)(2,1)S(1)} async-done(((bf16[32,8,512]{2,1,0:T(8,128)(2,1)}), bf16[32,8,512]{2,1,0:T(8,128)(2,1)S(1)}, u32[]{:S(2)}, u32[]{:S(2)}) %all-to-all-start.5) | async-done | bytes 262176 | tf_op jit(solution)/shard_map/all_to_all | solution.py:15
  172.1 3.7 %all-to-all-start.4 = ((bf16[16,8,4096]{2,1,0:T(8,128)(2,1)}), bf16[16,8,4096]{2,1,0:T(8,128)(2,1)S(1)}, u32[]{:S(2)}, u32[]{:S(2)}) async-start(bf16[16,8,4096]{2,1,0:T(8,128)(2,1)} %bitcast.94), calls=%async_computation.4 | async-start | bytes 2097152 | tf_op jit(solution)/shard_map/all_to_all | solution.py:15
  175.8 0.0 copy-done.4
  175.8 0.8 select_reduce_fusion.1
  176.5 0.1 select_reduce_fusion
  176.7 0.8 copy.66
  177.4 1.7 reshape.121
  179.2 0.4 fusion.82
  179.6 0.0 copy-start.2
  179.6 1.8 convolution_add_fusion.2
  181.5 0.0 copy-start.1
  181.5 18.8 %all-to-all-done.4 = bf16[16,8,4096]{2,1,0:T(8,128)(2,1)S(1)} async-done(((bf16[16,8,4096]{2,1,0:T(8,128)(2,1)}), bf16[16,8,4096]{2,1,0:T(8,128)(2,1)S(1)}, u32[]{:S(2)}, u32[]{:S(2)}) %all-to-all-start.4) | async-done | bytes 1048608 | tf_op jit(solution)/shard_map/all_to_all | solution.py:15
  200.3 0.0 copy-done.2
  200.3 0.4 fusion.49
  200.7 0.0 copy-done.1
  200.8 1.5 fusion.3
  (9 shorter events, 0.1 us)
Async XLA Ops:
  0.6 11.5 %copy-start.5 = (s32[128,2]{0,1:T(2,128)S(1)}, s32[128,2]{0,1:T(2,128)}, u32[]{:S(2)}) copy-start(s32[128,2]{0,1:T(2,128)} %param.12) | copy-start | bytes 3076
  0.6 12.2 %copy-start = (bf16[128,4096]{1,0:T(8,128)(2,1)S(1)}, bf16[128,4096]{1,0:T(8,128)(2,1)}, u32[]{:S(2)}) copy-start(bf16[128,4096]{1,0:T(8,128)(2,1)} %param.10) | copy-start | bytes 3145732
  0.7 12.6 %copy-start.3 = (f32[4096]{0:T(1024)S(1)}, f32[4096]{0:T(1024)}, u32[]{:S(2)}) copy-start(f32[4096]{0:T(1024)} %param.11) | copy-start | bytes 49156
  4.8 19.3 %all-to-all-start = ((bf16[32,8,640]{2,1,0:T(8,128)(2,1)}), bf16[32,8,640]{2,1,0:T(8,128)(2,1)S(1)}, u32[]{:S(2)}, u32[]{:S(2)}) async-start(bf16[32,8,640]{2,1,0:T(8,128)(2,1)} %copy.65), calls=%async_computation | async-start | bytes 655360 | tf_op jit(solution)/shard_map/all_to_all | solution.py:15
  24.1 46.8 %all-to-all-start.1 = ((bf16[16,16,4096]{2,1,0:T(8,128)(2,1)}), bf16[16,16,4096]{2,1,0:T(8,128)(2,1)S(1)}, u32[]{:S(2)}, u32[]{:S(2)}) async-start(bf16[16,16,4096]{2,1,0:T(8,128)(2,1)} %bitcast.93), calls=%async_computation.1 | async-start | bytes 4194304 | tf_op jit(solution)/shard_map/all_to_all | solution.py:15
  27.8 56.9 %collective-permute-start.1 = (bf16[1,4096,384]{2,1,0:T(8,128)(2,1)}, bf16[1,4096,384]{2,1,0:T(8,128)(2,1)}, u32[]{:S(2)}, u32[]{:S(2)}) collective-permute-start(bf16[1,4096,384]{2,1,0:T(8,128)(2,1)} %param.15), channel_id=1, source_target_pairs={{0,1},{1,0},{2,3},{3,2},{4,5},{5,4},{6,7},{7,6},{8,9},{9,8},{10,11... | collective-permute-start | bytes 9437192 | tf_op jit(solution)/shard_map/ppermute | solution.py:77
  27.9 68.0 %collective-permute-start = (bf16[1,4096,384]{2,1,0:T(8,128)(2,1)}, bf16[1,4096,384]{2,1,0:T(8,128)(2,1)}, u32[]{:S(2)}, u32[]{:S(2)}) collective-permute-start(bf16[1,4096,384]{2,1,0:T(8,128)(2,1)} %param.14), channel_id=1, source_target_pairs={{0,1},{1,0},{2,3},{3,2},{4,5},{5,4},{6,7},{7,6},{8,9},{9,8},{10,11... | collective-permute-start | bytes 9437192 | tf_op jit(solution)/shard_map/ppermute | solution.py:77
  28.4 67.5 %collective-permute-start.2 = (bf16[1,384,4096]{2,1,0:T(8,128)(2,1)}, bf16[1,384,4096]{2,1,0:T(8,128)(2,1)}, u32[]{:S(2)}, u32[]{:S(2)}) collective-permute-start(bf16[1,384,4096]{2,1,0:T(8,128)(2,1)} %param.16), channel_id=1, source_target_pairs={{0,1},{1,0},{2,3},{3,2},{4,5},{5,4},{6,7},{7,6},{8,9},{9,8},{10,11... | collective-permute-start | bytes 9437192 | tf_op jit(solution)/shard_map/ppermute | solution.py:77
  70.9 33.5 %all-to-all-start.2 = ((bf16[16,8,4096]{2,1,0:T(8,128)(2,1)}), bf16[16,8,4096]{2,1,0:T(8,128)(2,1)S(1)}, u32[]{:S(2)}, u32[]{:S(2)}) async-start(bf16[16,8,4096]{2,1,0:T(8,128)(2,1)} %fusion.4), calls=%async_computation.2 | async-start | bytes 2097152 | tf_op jit(solution)/shard_map/all_to_all | solution.py:15
  104.4 48.4 %all-to-all-start.3 = ((bf16[16,16,4096]{2,1,0:T(8,128)(2,1)}), bf16[16,16,4096]{2,1,0:T(8,128)(2,1)S(1)}, u32[]{:S(2)}, u32[]{:S(2)}) async-start(bf16[16,16,4096]{2,1,0:T(8,128)(2,1)} %bitcast.92), calls=%async_computation.3 | async-start | bytes 4194304 | tf_op jit(solution)/shard_map/all_to_all | solution.py:15
  152.8 19.3 %all-to-all-start.5 = ((bf16[32,8,512]{2,1,0:T(8,128)(2,1)}), bf16[32,8,512]{2,1,0:T(8,128)(2,1)S(1)}, u32[]{:S(2)}, u32[]{:S(2)}) async-start(bf16[32,8,512]{2,1,0:T(8,128)(2,1)} %fusion.36), calls=%async_computation.5 | async-start | bytes 524288 | tf_op jit(solution)/shard_map/all_to_all | solution.py:15
  167.4 8.3 %copy-start.4 = (f32[128,2]{0,1:T(2,128)S(1)}, f32[128,2]{0,1:T(2,128)}, u32[]{:S(2)}) copy-start(f32[128,2]{0,1:T(2,128)} %param.13) | copy-start | bytes 3076
  172.1 28.2 %all-to-all-start.4 = ((bf16[16,8,4096]{2,1,0:T(8,128)(2,1)}), bf16[16,8,4096]{2,1,0:T(8,128)(2,1)S(1)}, u32[]{:S(2)}, u32[]{:S(2)}) async-start(bf16[16,8,4096]{2,1,0:T(8,128)(2,1)} %bitcast.94), calls=%async_computation.4 | async-start | bytes 2097152 | tf_op jit(solution)/shard_map/all_to_all | solution.py:15
  179.6 20.7 %copy-start.2 = (f32[128,128]{1,0:T(8,128)S(1)}, f32[128,128]{1,0:T(8,128)}, u32[]{:S(2)}) copy-start(f32[128,128]{1,0:T(8,128)} %select_reduce_fusion.1) | copy-start | bytes 196612
  181.5 19.3 %copy-start.1 = (f32[128,4096]{1,0:T(8,128)S(1)}, f32[128,4096]{1,0:T(8,128)}, u32[]{:S(2)}) copy-start(f32[128,4096]{1,0:T(8,128)} %convolution_add_fusion.2) | copy-start | bytes 6291460

commit v4 on v3

--- a/solution.py
+++ b/solution.py
@@ -17,25 +17,39 @@
     )
 
 
-def pages_phase_one(kv_pages, page_table, kv_lengths, nodes):
-    pages_dev, page_len, kv_width = kv_pages.shape
-    piece = page_len * kv_width // nodes
-    live = jnp.arange(pages_dev, dtype=jnp.int32) < kv_lengths[0]
-    marks = jnp.stack([jnp.where(live, page_table[:, 0], -1), page_table[:, 1]], axis=1).astype(BF)
-    tail = jnp.broadcast_to(jnp.pad(marks, ((0, 0), (0, 126)))[None], (nodes, pages_dev, 128))
-    pieces = kv_pages.reshape(pages_dev, nodes, piece).swapaxes(0, 1)
-    sent = jnp.concatenate([pieces, tail], axis=2)
-    return all_to_all(sent).reshape(nodes * pages_dev, piece + 128)
+def by_core(core, pair):
+    first, second = pair
+    return jnp.where(core == 0, first, second), jnp.where(core == 0, second, first)
 
 
-def pages_phase_two(got, nodes, shape):
-    pages_dev = shape[0]
-    piece = got.shape[1] - 128
-    marks = got[:, piece : piece + 2].astype(jnp.int32)
+def pages_out(kv_pages, page_table, kv_lengths, core, swap, chips, rows):
+    pages_dev, page_len, kv_width = kv_pages.shape
+    live = jnp.arange(pages_dev, dtype=jnp.int32) < kv_lengths[0]
+    marks = jnp.stack([jnp.where(live, page_table[:, 0], -1), page_table[:, 1]], axis=1)
+    marks = jnp.concatenate([marks, lax.ppermute(marks, "node", swap)], axis=0)
+    split = kv_pages.reshape(pages_dev, chips, 2, -1)
+    keep, give = by_core(core, (split[:, :, 0], split[:, :, 1]))
+    pieces = jnp.concatenate([keep, lax.ppermute(give, "node", swap)], axis=0).swapaxes(0, 1)
+    tail = jnp.pad(marks.reshape(-1).astype(BF), (0, 128 - marks.size))
+    tail = jnp.broadcast_to(tail[None, None, :], (chips, rows, 128))
+    return jnp.concatenate([pieces.reshape(chips, rows, -1), tail], axis=2)
+
+
+def pages_place(got, pages_dev, chips, rows):
+    count = 2 * pages_dev
+    pieces = got[:, :, :-128].reshape(chips * count, -1)
+    marks = got[:, 0, -128:][:, : 2 * count].astype(jnp.int32).reshape(chips * count, 2)
     code = jnp.where(marks[:, 0] < 0, -1, marks[:, 0] * pages_dev + marks[:, 1])
     placing = (code[None, :] == jnp.arange(code.shape[0], dtype=jnp.int32)[:, None]).astype(BF)
-    sent = dot32(placing, got[:, :piece]).astype(BF).reshape(nodes, pages_dev, piece)
-    return all_to_all(sent)
+    return dot32(placing, pieces).astype(BF).reshape(chips, rows, -1)
+
+
+def pages_in(got, core, swap, shape):
+    pages_dev = shape[0]
+    got = got.reshape(got.shape[0], 2 * pages_dev, -1)
+    keep, give = by_core(core, (got[:, :pages_dev], got[:, pages_dev:]))
+    pair = by_core(core, (keep, lax.ppermute(give, "node", swap)))
+    return jnp.stack(pair, axis=1).transpose(2, 0, 1, 3).reshape(shape)
 
 
 def shards(
@@ -56,7 +70,11 @@
     top = expert_ids.shape[1]
     cap = tok_rows * top * 3 // (2 * experts)
 
-    page_pieces = pages_phase_one(kv_pages, page_table, kv_lengths, nodes)
+    core = lax.axis_index("node") % 2
+    swap = [(i, i ^ 1) for i in range(nodes)]
+    pages_dev = kv_pages.shape[0]
+    large = cap * 2 // 3
+    small = cap - large
 
     flat = expert_ids.reshape(-1)
     pairs = flat.shape[0]
@@ -70,7 +88,6 @@
     factor = lax.rsqrt(jnp.mean(values * values, axis=1, keepdims=True) + 1e-06)
     normed = (values * factor * norm_gain[None, :]).astype(BF)
 
-    swap = [(i, i ^ 1) for i in range(nodes)]
     parity = [list(range(c, nodes, 2)) for c in (0, 1)]
 
     def both(w):
@@ -91,7 +108,7 @@
         return rows.astype(BF).reshape(experts, count, width)
 
     def exchange(x):
-        return all_to_all(x.reshape(experts, -1, width), parity).reshape(-1, width)
+        return all_to_all(x, parity)
 
     def expert(x):
         total = None
@@ -107,21 +124,22 @@
         low = (scale - high.astype(F32)).astype(BF)
         return dot32(high, returned) + dot32(low, returned)
 
-    large = cap * 2 // 3
-    small = cap - large
-    one_out, page_pieces = lax.optimization_barrier((send(0, large), page_pieces))
-    one = exchange(one_out)
-    two_out, one = lax.optimization_barrier((send(large, small), one))
+    one = exchange(send(0, large)).reshape(-1, width)
+    pages = pages_out(kv_pages, page_table, kv_lengths, core, swap, experts, small)
+    two_out = jnp.concatenate([send(large, small), pages], axis=2)
+    two_out, one = lax.optimization_barrier((two_out, one))
     two = exchange(two_out)
-    one_done = expert(one)
-    slots = pages_phase_two(page_pieces, nodes, kv_pages.shape)
-    one_done, two = lax.optimization_barrier((one_done, two))
-    one_back = exchange(one_done)
-    two_done = expert(two)
+    one_done = expert(one).reshape(experts, large, width)
+    slots = pages_place(two[:, :, width:], pages_dev, experts, large)
+    two = two[:, :, :width].reshape(-1, width)
+    one_back = exchange(jnp.concatenate([one_done, slots], axis=2))
+    two_done = expert(two).reshape(experts, small, width)
     two_done, one_back = lax.optimization_barrier((two_done, one_back))
-    two_back = exchange(two_done)
+    two_back = exchange(two_done).reshape(-1, width)
+    decode_pages = pages_in(one_back[:, :, width:], core, swap, kv_pages.shape)
+    one_back = one_back[:, :, :width].reshape(-1, width)
     moe_output = (combine(0, large, one_back) + combine(large, small, two_back)).astype(BF)
-    return (moe_output, slots.swapaxes(0, 1).reshape(kv_pages.shape))
+    return (moe_output, decode_pages)
 
 
 def solution(mesh):

time: 203 us -> 193 us (0.951)
  waiting for transfers between devices: 103 us -> 85.3 us
  other arithmetic: 3.02 us -> 13.9 us
  starting transfers between devices: 40.3 us -> 36.9 us
  local copies, waits for them, and re-layouts: 5.07 us -> 7.14 us
    all_to_all x6 -> x4, waiting for transfers between devices: 103 us -> 84.9 us  [all_to_all(): lax.all_to_all(x, 'node', split_axis=0, concat_axis=0, axis_index_groups=...]
    concatenate x1 -> x4, other arithmetic: 0.03 us -> 5.62 us  [the longest x1 3.26 us: shards(): one_back = exchange(jnp.concatenate([one_done, slots], axis=2))]
    all_to_all x6 -> x4, starting transfers between devices: 39.6 us -> 35.6 us  [all_to_all(): lax.all_to_all(x, 'node', split_axis=0, concat_axis=0, axis_index_groups=...]
    dot_general x14, matrix products: 45.8 us -> 42.7 us  [dot32(): return jnp.dot(a, b, preferred_element_type=F32)]
  transfers between devices with their start and end apart: 9 -> 10, of which waited for: 6 -> 5; matrix products, arithmetic and copies ran while one was open for 26% -> 29% of each run, Pallas kernels for 0% -> 0%
where the time goes in v4:
time: 193 us; the launch traced here: 192 us
  waiting for transfers between devices  85.3 us (44%)
  matrix products  47.6 us (25%)
  starting transfers between devices  36.9 us (19%)
  other arithmetic  13.9 us (7%)
  local copies, waits for them, and re-layouts  7.14 us (4%)
    all_to_all x4, waiting for transfers between devices, all_to_all(): lax.all_to_all(x, 'node', split_axis=0, concat_axis=0, axis_index_groups=...  84.9 us
    dot_general x14, matrix products, dot32(): return jnp.dot(a, b, preferred_element_type=F32)  42.7 us
    all_to_all x4, starting transfers between devices, all_to_all(): lax.all_to_all(x, 'node', split_axis=0, concat_axis=0, axis_index_groups=...  35.6 us
    dot_general x2, matrix products, send(): lax.dot_general(placed, normed, (((0,), (0,)), ((), ())), preferred_eleme...  4.99 us
  transfers between devices with their start and end apart: 10, of which 5 were waited for; matrix products, arithmetic and copies ran while one was open for 29% of the time, Pallas kernels for 0%

profile of v4, /device:TPU:0, one launch (start us, length us, event | category | flops | bytes accessed | tf_op | source)
XLA Modules:
  0.0 192.5 jit_solution(15426410245070860491)
XLA Ops:
  0.6 1.6 fusion.28
  2.3 0.8 copy.63
  3.0 0.1 eq.28
  3.2 0.2 fusion.47
  3.4 0.1 convert_element_type.79
  3.5 0.1 copy.64
  3.6 1.3 and_select_fusion.1
  4.9 0.6 copy-done.3
  5.5 0.1 fusion.58
  5.6 2.8 %convolution_convert_fusion = bf16[256,4096]{1,0:T(8,128)(2,1)} fusion(pred[128,256]{1,0:T(8,128)(4,1)S(1)} %fusion.58, bf16[128,4096]{1,0:T(8,128)(2,1)S(1)} %copy-done, f32[4096]{0:T(1024)} %param.11, f32[128]{0:T(128)S(1)} %add_rsqrt_fusion), kind=kOutput, calls=%fused_computation.1 | convolution fusion | flops 271581184 | bytes 3195392 | tf_op jit(solution)/shard_map/dot_general | solution.py:105
  8.4 8.4 %all-to-all-start = ((bf16[16,16,4096]{2,1,0:T(8,128)(2,1)}), bf16[16,16,4096]{2,1,0:T(8,128)(2,1)S(1)}, u32[]{:S(2)}, u32[]{:S(2)}) async-start(bf16[16,16,4096]{2,1,0:T(8,128)(2,1)} %bitcast.110), calls=%async_computation | async-start | bytes 4194304 | tf_op jit(solution)/shard_map/all_to_all | solution.py:15
  16.9 0.1 collective-permute-start.3
  17.6 0.6 fusion.91
  18.2 0.5 collective-permute-start.1
  18.7 1.1 reshape.126
  19.9 0.6 broadcast_select_fusion.1
  20.5 0.1 collective-permute-start
  20.6 0.5 collective-permute-start.2
  21.1 0.1 collective-permute-start.4
  21.2 0.8 fusion.73
  22.0 2.2 %fusion.4 = bf16[16,8,4096]{2,1,0:T(8,128)(2,1)} fusion(pred[128,128]{1,0:T(8,128)(4,1)S(1)} %fusion.73, bf16[128,4096]{1,0:T(8,128)(2,1)S(1)} %copy-done, f32[4096]{0:T(1024)S(1)} %copy-done.2, f32[128]{0:T(128)} %copy-done.7), kind=kOutput, calls=%fused_computation.10 | convolution fusion | flops 136839168 | bytes 2130432 | tf_op jit(solution)/shard_map/dot_general | solution.py:105
  24.2 0.0 collective-permute-done.1
  24.2 0.7 convert.8
  24.9 0.1 pad_maximum_fusion.1
  25.0 0.1 copy.71
  25.1 0.1 convert_element_type.84
  25.2 0.0 collective-permute-done
  25.3 0.2 copy.70
  25.4 0.8 reshape.127
  26.2 2.3 %maximum_maximum_fusion = bf16[16,8,5248]{2,1,0:T(8,128)(2,1)} fusion(bf16[16,8,1024]{2,1,0:T(8,128)(2,1)} %reshape.127, bf16[16,8,4096]{2,1,0:T(8,128)(2,1)S(1)} %copy-done.1, bf16[5248]{0:T(1024)(128)(2,1)S(1)} %fusion.83), kind=kLoop, calls=%fused_computation.40 | loop fusion | flops 4030464 | bytes 2664704 | tf_op jit(solution)/shard_map/concatenate | solution.py:129
  28.5 31.5 %all-to-all-done = bf16[16,16,4096]{2,1,0:T(8,128)(2,1)S(1)} async-done(((bf16[16,16,4096]{2,1,0:T(8,128)(2,1)}), bf16[16,16,4096]{2,1,0:T(8,128)(2,1)S(1)}, u32[]{:S(2)}, u32[]{:S(2)}) %all-to-all-start) | async-done | bytes 2097184 | tf_op jit(solution)/shard_map/all_to_all | solution.py:15
  59.9 10.0 %all-to-all-start.1 = ((bf16[16,8,5248]{2,1,0:T(8,128)(2,1)}), bf16[16,8,5248]{2,1,0:T(8,128)(2,1)S(1)}, u32[]{:S(2)}, u32[]{:S(2)}) async-start(bf16[16,8,5248]{2,1,0:T(8,128)(2,1)} %maximum_maximum_fusion), calls=%async_computation.1 | async-start | bytes 2686976 | tf_op jit(solution)/shard_map/all_to_all | solution.py:15
  69.9 3.9 %fusion.24 = f32[256,384]{1,0:T(8,128)} fusion(bf16[256,4096]{1,0:T(8,128)(2,1)S(1)} %bitcast.103, bf16[1,4096,384]{2,1,0:T(8,128)(2,1)} %param.14), kind=kOutput, calls=%fused_computation.30 | convolution fusion | flops 805306368 | bytes 5636096 | tf_op jit(solution)/shard_map/dot_general | solution.py:11
  73.8 0.0 collective-permute-done.3
  73.8 3.9 %fusion.8 = f32[256,384]{1,0:T(8,128)} fusion(bf16[256,4096]{1,0:T(8,128)(2,1)S(1)} %bitcast.104, bf16[1,4096,384]{2,1,0:T(8,128)(2,1)} %collective-permute-done.3), kind=kOutput, calls=%fused_computation.14 | convolution fusion | flops 805306368 | bytes 5636096 | tf_op jit(solution)/shard_map/dot_general | solution.py:11
  77.7 7.3 %fusion.16 = f32[256,4096]{1,0:T(8,128)} fusion(bf16[1,384,4096]{2,1,0:T(8,128)(2,1)} %param.16, bf16[256,4096]{1,0:T(8,128)(2,1)S(1)} %bitcast.105, bf16[1,4096,384]{2,1,0:T(8,128)(2,1)} %param.15, f32[256,384]{1,0:T(8,128)} %fusion.24), kind=kOutput, calls=%fused_computation.22 | convolution fusion | flops 1611202560 | bytes 12976128 | tf_op jit(solution)/shard_map/dot_general | solution.py:11
  85.1 8.0 %fusion = bf16[256,4096]{1,0:T(8,128)(2,1)} fusion(f32[256,4096]{1,0:T(8,128)} %fusion.16, bf16[1,384,4096]{2,1,0:T(8,128)(2,1)} %collective-permute-done.4, f32[256,384]{1,0:T(8,128)} %fusion.8, bf16[256,4096]{1,0:T(8,128)(2,1)S(1)} %bitcast.106, bf16[1,4096,384]{2,1,0:T(8,128)(2,1)} %collective-permute-done.2), kind=kOutput, calls=%fused_computation.2 | convolution fusion | flops 1613299712 | bytes 15073280 | tf_op jit(solution)/shard_map/dot_general | solution.py:11
  93.0 6.2 %all-to-all-done.1 = bf16[16,8,5248]{2,1,0:T(8,128)(2,1)S(1)} async-done(((bf16[16,8,5248]{2,1,0:T(8,128)(2,1)}), bf16[16,8,5248]{2,1,0:T(8,128)(2,1)S(1)}, u32[]{:S(2)}, u32[]{:S(2)}) %all-to-all-start.1) | async-done | bytes 1343520 | tf_op jit(solution)/shard_map/all_to_all | solution.py:15
  99.3 0.1 reshape.141
  99.4 0.2 fusion.71
  99.6 0.1 reshape.135
  99.7 0.2 convolution_convert_fusion.2
  99.9 3.3 %pad_maximum_fusion = bf16[16,16,4608]{2,1,0:T(8,128)(2,1)} fusion(bf16[16,16,512]{2,1,0:T(8,128)(2,1)S(1)} %bitcast.111, bf16[16,16,4096]{2,1,0:T(8,128)(2,1)} %bitcast.109), kind=kLoop, calls=%fused_computation.36 | loop fusion | flops 4718592 | bytes 4718592 | tf_op jit(solution)/shard_map/concatenate | solution.py:135
  103.2 6.5 %all-to-all-start.2 = ((bf16[16,16,4608]{2,1,0:T(8,128)(2,1)}), bf16[16,16,4608]{2,1,0:T(8,128)(2,1)}, u32[]{:S(2)}, u32[]{:S(2)}) async-start(bf16[16,16,4608]{2,1,0:T(8,128)(2,1)} %pad_maximum_fusion), calls=%async_computation.2 | async-start | bytes 4718592 | tf_op jit(solution)/shard_map/all_to_all | solution.py:15
  109.7 3.3 %fusion.26 = f32[128,384]{1,0:T(8,128)} fusion(bf16[1,4096,384]{2,1,0:T(8,128)(2,1)} %param.14, bf16[16,8,5248]{2,1,0:T(8,128)(2,1)S(1)} %all-to-all-done.1), kind=kOutput, calls=%fused_computation.32 | convolution fusion | flops 402653184 | bytes 4390912 | tf_op jit(solution)/shard_map/dot_general | solution.py:11
  113.0 3.3 %fusion.10 = f32[128,384]{1,0:T(8,128)} fusion(bf16[1,4096,384]{2,1,0:T(8,128)(2,1)} %collective-permute-done.3, bf16[16,8,5248]{2,1,0:T(8,128)(2,1)S(1)} %all-to-all-done.1), kind=kOutput, calls=%fused_computation.16 | convolution fusion | flops 402653184 | bytes 4390912 | tf_op jit(solution)/shard_map/dot_general | solution.py:11
  116.2 4.3 %fusion.18 = f32[128,4096]{1,0:T(8,128)S(1)} fusion(bf16[1,384,4096]{2,1,0:T(8,128)(2,1)} %param.16, bf16[1,4096,384]{2,1,0:T(8,128)(2,1)} %param.15, bf16[16,8,5248]{2,1,0:T(8,128)(2,1)S(1)} %all-to-all-done.1, f32[128,384]{1,0:T(8,128)} %fusion.26), kind=kOutput, calls=%fused_computation.24 | convolution fusion | flops 805601280 | bytes 9633792 | tf_op jit(solution)/shard_map/dot_general | solution.py:11
  120.6 5.4 %fusion.5 = bf16[16,8,4096]{2,1,0:T(8,128)(2,1)} fusion(f32[128,4096]{1,0:T(8,128)S(1)} %fusion.18, bf16[1,384,4096]{2,1,0:T(8,128)(2,1)} %collective-permute-done.4, f32[128,384]{1,0:T(8,128)} %fusion.10, bf16[1,4096,384]{2,1,0:T(8,128)(2,1)} %collective-permute-done.2, bf16[16,8,5248]{2,1,0:T(8,128)(2,1)S(1)} %all-to-all-done.1), kind=kOutput, calls=%fused_computation.11 | convolution fusion | flops 806649856 | bytes 10682368 | tf_op jit(solution)/shard_map/dot_general | solution.py:11
  126.0 30.4 %all-to-all-done.2 = bf16[16,16,4608]{2,1,0:T(8,128)(2,1)} async-done(((bf16[16,16,4608]{2,1,0:T(8,128)(2,1)}), bf16[16,16,4608]{2,1,0:T(8,128)(2,1)}, u32[]{:S(2)}, u32[]{:S(2)}) %all-to-all-start.2) | async-done | bytes 2359328 | tf_op jit(solution)/shard_map/all_to_all | solution.py:15
  156.4 10.8 %all-to-all-start.3 = ((bf16[16,8,4096]{2,1,0:T(8,128)(2,1)}), bf16[16,8,4096]{2,1,0:T(8,128)(2,1)S(1)}, u32[]{:S(2)}, u32[]{:S(2)}) async-start(bf16[16,8,4096]{2,1,0:T(8,128)(2,1)} %fusion.5), calls=%async_computation.3 | async-start | bytes 2097152 | tf_op jit(solution)/shard_map/all_to_all | solution.py:15
  167.2 0.1 select_reduce_fusion.1
  167.4 0.1 select_reduce_fusion
  167.5 1.7 slice.56
  169.2 1.0 broadcast_select_fusion.2
  170.2 0.1 collective-permute-start.5
  170.3 0.4 fusion.81
  170.8 0.5 convolution_add_fusion.2
  171.3 0.4 collective-permute-done.5
  171.7 1.0 select_bitcast_fusion.1
  172.7 0.3 copy.72
  173.0 0.9 reshape.139
  173.8 16.7 %all-to-all-done.3 = bf16[16,8,4096]{2,1,0:T(8,128)(2,1)S(1)} async-done(((bf16[16,8,4096]{2,1,0:T(8,128)(2,1)}), bf16[16,8,4096]{2,1,0:T(8,128)(2,1)S(1)}, u32[]{:S(2)}, u32[]{:S(2)}) %all-to-all-start.3) | async-done | bytes 1048608 | tf_op jit(solution)/shard_map/all_to_all | solution.py:15
  190.6 0.4 fusion.49
  191.0 1.5 fusion.3
  (33 shorter events, 0.2 us)
Async XLA Ops:
  0.6 4.9 %copy-start = (bf16[128,4096]{1,0:T(8,128)(2,1)S(1)}, bf16[128,4096]{1,0:T(8,128)(2,1)}, u32[]{:S(2)}) copy-start(bf16[128,4096]{1,0:T(8,128)(2,1)} %param.10) | copy-start | bytes 3145732
  2.3 6.2 %copy-start.7 = (f32[128]{0:T(128)}, f32[128]{0:T(128)S(1)}, u32[]{:S(2)}) copy-start(f32[128]{0:T(128)S(1)} %add_rsqrt_fusion) | copy-start | bytes 1540
  4.9 0.6 copy-start.3
  8.4 9.2 %copy-start.8 = (s32[8,2]{0,1:T(2,128)S(1)}, s32[8,2]{0,1:T(2,128)}, u32[]{:S(2)}) copy-start(s32[8,2]{0,1:T(2,128)} %param.18) | copy-start | bytes 196
  8.4 13.6 %copy-start.2 = (f32[4096]{0:T(1024)S(1)}, f32[4096]{0:T(1024)}, u32[]{:S(2)}) copy-start(f32[4096]{0:T(1024)} %param.11) | copy-start | bytes 49156
  8.4 51.5 %all-to-all-start = ((bf16[16,16,4096]{2,1,0:T(8,128)(2,1)}), bf16[16,16,4096]{2,1,0:T(8,128)(2,1)S(1)}, u32[]{:S(2)}, u32[]{:S(2)}) async-start(bf16[16,16,4096]{2,1,0:T(8,128)(2,1)} %bitcast.110), calls=%async_computation | async-start | bytes 4194304 | tf_op jit(solution)/shard_map/all_to_all | solution.py:15
  16.9 56.9 %collective-permute-start.3 = (bf16[1,4096,384]{2,1,0:T(8,128)(2,1)}, bf16[1,4096,384]{2,1,0:T(8,128)(2,1)}, u32[]{:S(2)}, u32[]{:S(2)}) collective-permute-start(bf16[1,4096,384]{2,1,0:T(8,128)(2,1)} %param.15), channel_id=1, source_target_pairs={{0,1},{1,0},{2,3},{3,2},{4,5},{5,4},{6,7},{7,6},{8,9},{9,8},{10,11... | collective-permute-start | bytes 9437192 | tf_op jit(solution)/shard_map/ppermute | solution.py:94
  18.2 5.9 %collective-permute-start.1 = (s32[8,2]{0,1:T(2,128)}, s32[8,2]{0,1:T(2,128)}, u32[]{:S(2)}, u32[]{:S(2)}) collective-permute-start(s32[8,2]{0,1:T(2,128)} %get-tuple-element.17), channel_id=1, source_target_pairs={{0,1},{1,0},{2,3},{3,2},{4,5},{5,4},{6,7},{7,6},{8,9},{9,8},{10,11... | collective-permute-start | bytes 200 | tf_op jit(solution)/shard_map/ppermute | solution.py:29
  19.9 5.0 %copy-start.9 = (bf16[8,2]{0,1:T(2,128)(2,1)S(1)}, bf16[8,2]{0,1:T(2,128)(2,1)}, u32[]{:S(2)}) copy-start(bf16[8,2]{0,1:T(2,128)(2,1)} %get-tuple-element.16) | copy-start | bytes 100
  20.5 4.7 %collective-permute-start = (bf16[8,16,512]{2,1,0:T(8,128)(2,1)S(1)}, bf16[8,16,512]{2,1,0:T(8,128)(2,1)S(1)}, u32[]{:S(2)}, u32[]{:S(2)}) collective-permute-start(bf16[8,16,512]{2,1,0:T(8,128)(2,1)S(1)} %bitcast.113), channel_id=1, source_target_pairs={{0,1},{1,0},{2,3},{3,2},{4,5},{5,4},{6,7},{7,6},{8,9},{9,8},{10,11... | collective-permute-start | bytes 393224 | tf_op jit(solution)/shard_map/ppermute | solution.py:32
  20.6 64.4 %collective-permute-start.2 = (bf16[1,4096,384]{2,1,0:T(8,128)(2,1)}, bf16[1,4096,384]{2,1,0:T(8,128)(2,1)}, u32[]{:S(2)}, u32[]{:S(2)}) collective-permute-start(bf16[1,4096,384]{2,1,0:T(8,128)(2,1)} %param.14), channel_id=1, source_target_pairs={{0,1},{1,0},{2,3},{3,2},{4,5},{5,4},{6,7},{7,6},{8,9},{9,8},{10,11... | collective-permute-start | bytes 9437192 | tf_op jit(solution)/shard_map/ppermute | solution.py:94
  21.1 63.9 %collective-permute-start.4 = (bf16[1,384,4096]{2,1,0:T(8,128)(2,1)}, bf16[1,384,4096]{2,1,0:T(8,128)(2,1)}, u32[]{:S(2)}, u32[]{:S(2)}) collective-permute-start(bf16[1,384,4096]{2,1,0:T(8,128)(2,1)} %param.16), channel_id=1, source_target_pairs={{0,1},{1,0},{2,3},{3,2},{4,5},{5,4},{6,7},{7,6},{8,9},{9,8},{10,11... | collective-permute-start | bytes 9437192 | tf_op jit(solution)/shard_map/ppermute | solution.py:94
  24.1 2.1 %copy-start.1 = (bf16[16,8,4096]{2,1,0:T(8,128)(2,1)S(1)}, bf16[16,8,4096]{2,1,0:T(8,128)(2,1)}, u32[]{:S(2)}) copy-start(bf16[16,8,4096]{2,1,0:T(8,128)(2,1)} %fusion.4) | copy-start | bytes 3145732
  59.9 39.3 %all-to-all-start.1 = ((bf16[16,8,5248]{2,1,0:T(8,128)(2,1)}), bf16[16,8,5248]{2,1,0:T(8,128)(2,1)S(1)}, u32[]{:S(2)}, u32[]{:S(2)}) async-start(bf16[16,8,5248]{2,1,0:T(8,128)(2,1)} %maximum_maximum_fusion), calls=%async_computation.1 | async-start | bytes 2686976 | tf_op jit(solution)/shard_map/all_to_all | solution.py:15
  103.2 53.2 %all-to-all-start.2 = ((bf16[16,16,4608]{2,1,0:T(8,128)(2,1)}), bf16[16,16,4608]{2,1,0:T(8,128)(2,1)}, u32[]{:S(2)}, u32[]{:S(2)}) async-start(bf16[16,16,4608]{2,1,0:T(8,128)(2,1)} %pad_maximum_fusion), calls=%async_computation.2 | async-start | bytes 4718592 | tf_op jit(solution)/shard_map/all_to_all | solution.py:15
  125.9 41.3 %copy-start.5 = (s32[128,2]{0,1:T(2,128)S(1)}, s32[128,2]{0,1:T(2,128)}, u32[]{:S(2)}) copy-start(s32[128,2]{0,1:T(2,128)} %get-tuple-element.15) | copy-start | bytes 3076
  126.0 41.3 %copy-start.6 = (f32[128,2]{0,1:T(2,128)S(1)}, f32[128,2]{0,1:T(2,128)}, u32[]{:S(2)}) copy-start(f32[128,2]{0,1:T(2,128)} %param.13) | copy-start | bytes 3076
  126.0 41.4 %copy-start.4 = (s32[128,2]{0,1:T(2,128)S(1)}, s32[128,2]{0,1:T(2,128)}, u32[]{:S(2)}) copy-start(s32[128,2]{0,1:T(2,128)} %copy-done.3) | copy-start | bytes 3076
  156.4 34.2 %all-to-all-start.3 = ((bf16[16,8,4096]{2,1,0:T(8,128)(2,1)}), bf16[16,8,4096]{2,1,0:T(8,128)(2,1)S(1)}, u32[]{:S(2)}, u32[]{:S(2)}) async-start(bf16[16,8,4096]{2,1,0:T(8,128)(2,1)} %fusion.5), calls=%async_computation.3 | async-start | bytes 2097152 | tf_op jit(solution)/shard_map/all_to_all | solution.py:15
  170.2 1.4 collective-permute-start.5

commit v5 on v4

--- a/solution.py
+++ b/solution.py
@@ -130,9 +130,11 @@
     two_out, one = lax.optimization_barrier((two_out, one))
     two = exchange(two_out)
     one_done = expert(one).reshape(experts, large, width)
+    extra = 2 * kv_pages.size // (nodes * large)
+    one_done = lax.optimization_barrier(jnp.pad(one_done, ((0, 0), (0, 0), (0, extra))))
     slots = pages_place(two[:, :, width:], pages_dev, experts, large)
     two = two[:, :, :width].reshape(-1, width)
-    one_back = exchange(jnp.concatenate([one_done, slots], axis=2))
+    one_back = exchange(lax.dynamic_update_slice(one_done, slots, (0, 0, width)))
     two_done = expert(two).reshape(experts, small, width)
     two_done, one_back = lax.optimization_barrier((two_done, one_back))
     two_back = exchange(two_done).reshape(-1, width)

time: 193 us -> 191 us (0.990)
  local copies, waits for them, and re-layouts: 7.14 us -> 11.1 us
  other arithmetic: 13.9 us -> 10.6 us
  waiting for transfers between devices: 85.3 us -> 82 us
    concatenate x1 -> x0, other arithmetic: 3.26 us -> none  [shards(): one_back = exchange(jnp.concatenate([one_done, slots], axis=2))]
    all_to_all x4, waiting for transfers between devices: 84.9 us -> 81.6 us  [all_to_all(): lax.all_to_all(x, 'node', split_axis=0, concat_axis=0, axis_index_groups=...]
    pad x0 -> x1, local copies, waits for them, and re-layouts: none -> 3.2 us  [shards(): jnp.pad(one_done, ((0, 0), (0, 0), (0, extra)))]
  transfers between devices with their start and end apart: 10 -> 10, of which waited for: 5 -> 5; matrix products, arithmetic and copies ran while one was open for 29% -> 31% of each run, Pallas kernels for 0% -> 0%
where the time goes in v5:
time: 191 us; the launch traced here: 190 us
  waiting for transfers between devices  82 us (43%)
  matrix products  47.7 us (25%)
  starting transfers between devices  37 us (19%)
  local copies, waits for them, and re-layouts  11.1 us (6%)
  other arithmetic  10.6 us (6%)
    all_to_all x4, waiting for transfers between devices, all_to_all(): lax.all_to_all(x, 'node', split_axis=0, concat_axis=0, axis_index_groups=...  81.6 us
    dot_general x14, matrix products, dot32(): return jnp.dot(a, b, preferred_element_type=F32)  42.7 us
    all_to_all x4, starting transfers between devices, all_to_all(): lax.all_to_all(x, 'node', split_axis=0, concat_axis=0, axis_index_groups=...  35.7 us
    dot_general x2, matrix products, send(): lax.dot_general(placed, normed, (((0,), (0,)), ((), ())), preferred_eleme...  5.03 us
  transfers between devices with their start and end apart: 10, of which 5 were waited for; matrix products, arithmetic and copies ran while one was open for 31% of the time, Pallas kernels for 0%

profile of v5, /device:TPU:0, one launch (start us, length us, event | category | flops | bytes accessed | tf_op | source)
XLA Modules:
  0.0 190.0 jit_solution(14913847346918436914)
XLA Ops:
  0.6 1.6 fusion.28
  2.3 0.8 copy.63
  3.0 0.1 eq.28
  3.2 0.2 fusion.47
  3.4 0.1 convert_element_type.81
  3.5 0.1 copy.64
  3.6 1.3 and_select_fusion.1
  4.9 0.6 copy-done.3
  5.5 0.1 fusion.58
  5.6 2.9 %convolution_convert_fusion = bf16[256,4096]{1,0:T(8,128)(2,1)} fusion(pred[128,256]{1,0:T(8,128)(4,1)S(1)} %fusion.58, bf16[128,4096]{1,0:T(8,128)(2,1)S(1)} %copy-done, f32[4096]{0:T(1024)} %param.11, f32[128]{0:T(128)S(1)} %add_rsqrt_fusion), kind=kOutput, calls=%fused_computation.1 | convolution fusion | flops 271581184 | bytes 3195392 | tf_op jit(solution)/shard_map/dot_general | solution.py:105
  8.5 8.4 %all-to-all-start = ((bf16[16,16,4096]{2,1,0:T(8,128)(2,1)}), bf16[16,16,4096]{2,1,0:T(8,128)(2,1)S(1)}, u32[]{:S(2)}, u32[]{:S(2)}) async-start(bf16[16,16,4096]{2,1,0:T(8,128)(2,1)} %bitcast.110), calls=%async_computation | async-start | bytes 4194304 | tf_op jit(solution)/shard_map/all_to_all | solution.py:15
  16.9 0.1 collective-permute-start.3
  17.7 0.6 fusion.91
  18.3 0.5 collective-permute-start.1
  18.8 1.1 reshape.126
  19.9 0.6 broadcast_select_fusion.1
  20.6 0.1 collective-permute-start
  20.7 0.5 collective-permute-start.2
  21.2 0.1 collective-permute-start.4
  21.2 0.8 fusion.73
  22.0 2.2 %fusion.4 = bf16[16,8,4096]{2,1,0:T(8,128)(2,1)} fusion(pred[128,128]{1,0:T(8,128)(4,1)S(1)} %fusion.73, bf16[128,4096]{1,0:T(8,128)(2,1)S(1)} %copy-done, f32[4096]{0:T(1024)S(1)} %copy-done.2, f32[128]{0:T(128)} %copy-done.7), kind=kOutput, calls=%fused_computation.10 | convolution fusion | flops 136839168 | bytes 2130432 | tf_op jit(solution)/shard_map/dot_general | solution.py:105
  24.2 0.8 convert.8
  25.0 0.1 pad_maximum_fusion
  25.1 0.1 copy.71
  25.2 0.1 convert_element_type.86
  25.3 0.0 collective-permute-done
  25.3 0.2 copy.70
  25.5 0.8 reshape.127
  26.3 2.3 %maximum_maximum_fusion = bf16[16,8,5248]{2,1,0:T(8,128)(2,1)} fusion(bf16[16,8,1024]{2,1,0:T(8,128)(2,1)} %reshape.127, bf16[16,8,4096]{2,1,0:T(8,128)(2,1)S(1)} %copy-done.1, bf16[5248]{0:T(1024)(128)(2,1)S(1)} %fusion.83), kind=kLoop, calls=%fused_computation.39 | loop fusion | flops 4030464 | bytes 2664704 | tf_op jit(solution)/shard_map/concatenate | solution.py:129
  28.5 31.5 %all-to-all-done = bf16[16,16,4096]{2,1,0:T(8,128)(2,1)S(1)} async-done(((bf16[16,16,4096]{2,1,0:T(8,128)(2,1)}), bf16[16,16,4096]{2,1,0:T(8,128)(2,1)S(1)}, u32[]{:S(2)}, u32[]{:S(2)}) %all-to-all-start) | async-done | bytes 2097184 | tf_op jit(solution)/shard_map/all_to_all | solution.py:15
  60.0 10.0 %all-to-all-start.1 = ((bf16[16,8,5248]{2,1,0:T(8,128)(2,1)}), bf16[16,8,5248]{2,1,0:T(8,128)(2,1)S(1)}, u32[]{:S(2)}, u32[]{:S(2)}) async-start(bf16[16,8,5248]{2,1,0:T(8,128)(2,1)} %maximum_maximum_fusion), calls=%async_computation.1 | async-start | bytes 2686976 | tf_op jit(solution)/shard_map/all_to_all | solution.py:15
  70.0 3.9 %fusion.24 = f32[256,384]{1,0:T(8,128)} fusion(bf16[256,4096]{1,0:T(8,128)(2,1)S(1)} %bitcast.103, bf16[1,4096,384]{2,1,0:T(8,128)(2,1)} %param.14), kind=kOutput, calls=%fused_computation.30 | convolution fusion | flops 805306368 | bytes 5636096 | tf_op jit(solution)/shard_map/dot_general | solution.py:11
  73.9 0.0 collective-permute-done.3
  73.9 3.9 %fusion.8 = f32[256,384]{1,0:T(8,128)} fusion(bf16[256,4096]{1,0:T(8,128)(2,1)S(1)} %bitcast.104, bf16[1,4096,384]{2,1,0:T(8,128)(2,1)} %collective-permute-done.3), kind=kOutput, calls=%fused_computation.14 | convolution fusion | flops 805306368 | bytes 5636096 | tf_op jit(solution)/shard_map/dot_general | solution.py:11
  77.8 7.4 %fusion.16 = f32[256,4096]{1,0:T(8,128)} fusion(bf16[1,384,4096]{2,1,0:T(8,128)(2,1)} %param.16, bf16[256,4096]{1,0:T(8,128)(2,1)S(1)} %bitcast.105, bf16[1,4096,384]{2,1,0:T(8,128)(2,1)} %param.15, f32[256,384]{1,0:T(8,128)} %fusion.24), kind=kOutput, calls=%fused_computation.22 | convolution fusion | flops 1611202560 | bytes 12976128 | tf_op jit(solution)/shard_map/dot_general | solution.py:11
  85.1 8.0 %fusion = bf16[256,4096]{1,0:T(8,128)(2,1)} fusion(f32[256,4096]{1,0:T(8,128)} %fusion.16, bf16[1,384,4096]{2,1,0:T(8,128)(2,1)} %collective-permute-done.4, f32[256,384]{1,0:T(8,128)} %fusion.8, bf16[256,4096]{1,0:T(8,128)(2,1)S(1)} %bitcast.106, bf16[1,4096,384]{2,1,0:T(8,128)(2,1)} %collective-permute-done.2), kind=kOutput, calls=%fused_computation.2 | convolution fusion | flops 1613299712 | bytes 15073280 | tf_op jit(solution)/shard_map/dot_general | solution.py:11
  93.1 3.2 %pad.9 = bf16[16,16,4608]{2,1,0:T(8,128)(2,1)} pad(bf16[16,16,4096]{2,1,0:T(8,128)(2,1)} %bitcast.109, bf16[]{:T(256)} %constant.48.clone.1), padding=0_0x0_0x0_512 | pad | bytes 4456450 | tf_op jit(solution)/shard_map/jit(_pad)/pad | solution.py:134
  96.3 3.0 %all-to-all-done.1 = bf16[16,8,5248]{2,1,0:T(8,128)(2,1)S(1)} async-done(((bf16[16,8,5248]{2,1,0:T(8,128)(2,1)}), bf16[16,8,5248]{2,1,0:T(8,128)(2,1)S(1)}, u32[]{:S(2)}, u32[]{:S(2)}) %all-to-all-start.1) | async-done | bytes 1343520 | tf_op jit(solution)/shard_map/all_to_all | solution.py:15
  99.4 0.1 reshape.141
  99.5 0.2 fusion.71
  99.7 0.1 reshape.135
  99.8 0.2 convolution_convert_fusion.2
  100.0 0.8 constant_dynamic-update-slice_fusion
  100.8 6.5 %all-to-all-start.2 = ((bf16[16,16,4608]{2,1,0:T(8,128)(2,1)}), bf16[16,16,4608]{2,1,0:T(8,128)(2,1)}, u32[]{:S(2)}, u32[]{:S(2)}) async-start(bf16[16,16,4608]{2,1,0:T(8,128)(2,1)} %constant_dynamic-update-slice_fusion), calls=%async_computation.2 | async-start | bytes 4718592 | tf_op jit(solution)/shard_map/all_to_all | solution.py:15
  107.2 3.3 %fusion.26 = f32[128,384]{1,0:T(8,128)} fusion(bf16[1,4096,384]{2,1,0:T(8,128)(2,1)} %param.14, bf16[16,8,5248]{2,1,0:T(8,128)(2,1)S(1)} %all-to-all-done.1), kind=kOutput, calls=%fused_computation.32 | convolution fusion | flops 402653184 | bytes 4390912 | tf_op jit(solution)/shard_map/dot_general | solution.py:11
  110.5 3.3 %fusion.10 = f32[128,384]{1,0:T(8,128)} fusion(bf16[1,4096,384]{2,1,0:T(8,128)(2,1)} %collective-permute-done.3, bf16[16,8,5248]{2,1,0:T(8,128)(2,1)S(1)} %all-to-all-done.1), kind=kOutput, calls=%fused_computation.16 | convolution fusion | flops 402653184 | bytes 4390912 | tf_op jit(solution)/shard_map/dot_general | solution.py:11
  113.8 4.3 %fusion.18 = f32[128,4096]{1,0:T(8,128)S(1)} fusion(bf16[1,384,4096]{2,1,0:T(8,128)(2,1)} %param.16, bf16[1,4096,384]{2,1,0:T(8,128)(2,1)} %param.15, bf16[16,8,5248]{2,1,0:T(8,128)(2,1)S(1)} %all-to-all-done.1, f32[128,384]{1,0:T(8,128)} %fusion.26), kind=kOutput, calls=%fused_computation.24 | convolution fusion | flops 805601280 | bytes 9633792 | tf_op jit(solution)/shard_map/dot_general | solution.py:11
  118.2 5.4 %fusion.5 = bf16[16,8,4096]{2,1,0:T(8,128)(2,1)} fusion(f32[128,4096]{1,0:T(8,128)S(1)} %fusion.18, bf16[1,384,4096]{2,1,0:T(8,128)(2,1)} %collective-permute-done.4, f32[128,384]{1,0:T(8,128)} %fusion.10, bf16[1,4096,384]{2,1,0:T(8,128)(2,1)} %collective-permute-done.2, bf16[16,8,5248]{2,1,0:T(8,128)(2,1)S(1)} %all-to-all-done.1), kind=kOutput, calls=%fused_computation.11 | convolution fusion | flops 806649856 | bytes 10682368 | tf_op jit(solution)/shard_map/dot_general | solution.py:11
  123.5 30.4 %all-to-all-done.2 = bf16[16,16,4608]{2,1,0:T(8,128)(2,1)} async-done(((bf16[16,16,4608]{2,1,0:T(8,128)(2,1)}), bf16[16,16,4608]{2,1,0:T(8,128)(2,1)}, u32[]{:S(2)}, u32[]{:S(2)}) %all-to-all-start.2) | async-done | bytes 2359328 | tf_op jit(solution)/shard_map/all_to_all | solution.py:15
  154.0 10.8 %all-to-all-start.3 = ((bf16[16,8,4096]{2,1,0:T(8,128)(2,1)}), bf16[16,8,4096]{2,1,0:T(8,128)(2,1)S(1)}, u32[]{:S(2)}, u32[]{:S(2)}) async-start(bf16[16,8,4096]{2,1,0:T(8,128)(2,1)} %fusion.5), calls=%async_computation.3 | async-start | bytes 2097152 | tf_op jit(solution)/shard_map/all_to_all | solution.py:15
  164.8 0.1 select_reduce_fusion.1
  164.9 0.1 select_reduce_fusion
  165.1 1.7 slice.56
  166.8 1.0 broadcast_select_fusion.2
  167.8 0.1 collective-permute-start.5
  167.9 0.4 fusion.81
  168.3 0.5 convolution_add_fusion.2
  168.8 0.4 collective-permute-done.5
  169.2 1.0 select_bitcast_fusion.1
  170.2 0.3 copy.72
  170.5 0.9 reshape.139
  171.4 16.7 %all-to-all-done.3 = bf16[16,8,4096]{2,1,0:T(8,128)(2,1)S(1)} async-done(((bf16[16,8,4096]{2,1,0:T(8,128)(2,1)}), bf16[16,8,4096]{2,1,0:T(8,128)(2,1)S(1)}, u32[]{:S(2)}, u32[]{:S(2)}) %all-to-all-start.3) | async-done | bytes 1048608 | tf_op jit(solution)/shard_map/all_to_all | solution.py:15
  188.1 0.4 fusion.49
  188.5 1.5 fusion.3
  (34 shorter events, 0.2 us)
Async XLA Ops:
  0.6 5.0 %copy-start = (bf16[128,4096]{1,0:T(8,128)(2,1)S(1)}, bf16[128,4096]{1,0:T(8,128)(2,1)}, u32[]{:S(2)}) copy-start(bf16[128,4096]{1,0:T(8,128)(2,1)} %param.10) | copy-start | bytes 3145732
  2.3 6.2 %copy-start.7 = (f32[128]{0:T(128)}, f32[128]{0:T(128)S(1)}, u32[]{:S(2)}) copy-start(f32[128]{0:T(128)S(1)} %add_rsqrt_fusion) | copy-start | bytes 1540
  4.9 0.6 copy-start.3
  8.5 9.2 %copy-start.8 = (s32[8,2]{0,1:T(2,128)S(1)}, s32[8,2]{0,1:T(2,128)}, u32[]{:S(2)}) copy-start(s32[8,2]{0,1:T(2,128)} %param.18) | copy-start | bytes 196
  8.5 13.6 %copy-start.2 = (f32[4096]{0:T(1024)S(1)}, f32[4096]{0:T(1024)}, u32[]{:S(2)}) copy-start(f32[4096]{0:T(1024)} %param.11) | copy-start | bytes 49156
  8.5 51.5 %all-to-all-start = ((bf16[16,16,4096]{2,1,0:T(8,128)(2,1)}), bf16[16,16,4096]{2,1,0:T(8,128)(2,1)S(1)}, u32[]{:S(2)}, u32[]{:S(2)}) async-start(bf16[16,16,4096]{2,1,0:T(8,128)(2,1)} %bitcast.110), calls=%async_computation | async-start | bytes 4194304 | tf_op jit(solution)/shard_map/all_to_all | solution.py:15
  16.9 56.9 %collective-permute-start.3 = (bf16[1,4096,384]{2,1,0:T(8,128)(2,1)}, bf16[1,4096,384]{2,1,0:T(8,128)(2,1)}, u32[]{:S(2)}, u32[]{:S(2)}) collective-permute-start(bf16[1,4096,384]{2,1,0:T(8,128)(2,1)} %param.15), channel_id=1, source_target_pairs={{0,1},{1,0},{2,3},{3,2},{4,5},{5,4},{6,7},{7,6},{8,9},{9,8},{10,11... | collective-permute-start | bytes 9437192 | tf_op jit(solution)/shard_map/ppermute | solution.py:94
  18.3 5.9 %collective-permute-start.1 = (s32[8,2]{0,1:T(2,128)}, s32[8,2]{0,1:T(2,128)}, u32[]{:S(2)}, u32[]{:S(2)}) collective-permute-start(s32[8,2]{0,1:T(2,128)} %get-tuple-element.17), channel_id=1, source_target_pairs={{0,1},{1,0},{2,3},{3,2},{4,5},{5,4},{6,7},{7,6},{8,9},{9,8},{10,11... | collective-permute-start | bytes 200 | tf_op jit(solution)/shard_map/ppermute | solution.py:29
  19.9 5.1 %copy-start.9 = (bf16[8,2]{0,1:T(2,128)(2,1)S(1)}, bf16[8,2]{0,1:T(2,128)(2,1)}, u32[]{:S(2)}) copy-start(bf16[8,2]{0,1:T(2,128)(2,1)} %get-tuple-element.16) | copy-start | bytes 100
  20.6 4.7 %collective-permute-start = (bf16[8,16,512]{2,1,0:T(8,128)(2,1)S(1)}, bf16[8,16,512]{2,1,0:T(8,128)(2,1)S(1)}, u32[]{:S(2)}, u32[]{:S(2)}) collective-permute-start(bf16[8,16,512]{2,1,0:T(8,128)(2,1)S(1)} %bitcast.113), channel_id=1, source_target_pairs={{0,1},{1,0},{2,3},{3,2},{4,5},{5,4},{6,7},{7,6},{8,9},{9,8},{10,11... | collective-permute-start | bytes 393224 | tf_op jit(solution)/shard_map/ppermute | solution.py:32
  20.7 64.5 %collective-permute-start.2 = (bf16[1,4096,384]{2,1,0:T(8,128)(2,1)}, bf16[1,4096,384]{2,1,0:T(8,128)(2,1)}, u32[]{:S(2)}, u32[]{:S(2)}) collective-permute-start(bf16[1,4096,384]{2,1,0:T(8,128)(2,1)} %param.14), channel_id=1, source_target_pairs={{0,1},{1,0},{2,3},{3,2},{4,5},{5,4},{6,7},{7,6},{8,9},{9,8},{10,11... | collective-permute-start | bytes 9437192 | tf_op jit(solution)/shard_map/ppermute | solution.py:94
  21.2 64.0 %collective-permute-start.4 = (bf16[1,384,4096]{2,1,0:T(8,128)(2,1)}, bf16[1,384,4096]{2,1,0:T(8,128)(2,1)}, u32[]{:S(2)}, u32[]{:S(2)}) collective-permute-start(bf16[1,384,4096]{2,1,0:T(8,128)(2,1)} %param.16), channel_id=1, source_target_pairs={{0,1},{1,0},{2,3},{3,2},{4,5},{5,4},{6,7},{7,6},{8,9},{9,8},{10,11... | collective-permute-start | bytes 9437192 | tf_op jit(solution)/shard_map/ppermute | solution.py:94
  24.2 2.1 %copy-start.1 = (bf16[16,8,4096]{2,1,0:T(8,128)(2,1)S(1)}, bf16[16,8,4096]{2,1,0:T(8,128)(2,1)}, u32[]{:S(2)}) copy-start(bf16[16,8,4096]{2,1,0:T(8,128)(2,1)} %fusion.4) | copy-start | bytes 3145732
  60.0 39.3 %all-to-all-start.1 = ((bf16[16,8,5248]{2,1,0:T(8,128)(2,1)}), bf16[16,8,5248]{2,1,0:T(8,128)(2,1)S(1)}, u32[]{:S(2)}, u32[]{:S(2)}) async-start(bf16[16,8,5248]{2,1,0:T(8,128)(2,1)} %maximum_maximum_fusion), calls=%async_computation.1 | async-start | bytes 2686976 | tf_op jit(solution)/shard_map/all_to_all | solution.py:15
  100.8 53.2 %all-to-all-start.2 = ((bf16[16,16,4608]{2,1,0:T(8,128)(2,1)}), bf16[16,16,4608]{2,1,0:T(8,128)(2,1)}, u32[]{:S(2)}, u32[]{:S(2)}) async-start(bf16[16,16,4608]{2,1,0:T(8,128)(2,1)} %constant_dynamic-update-slice_fusion), calls=%async_computation.2 | async-start | bytes 4718592 | tf_op jit(solution)/shard_map/all_to_all | solution.py:15
  123.5 41.3 %copy-start.5 = (s32[128,2]{0,1:T(2,128)S(1)}, s32[128,2]{0,1:T(2,128)}, u32[]{:S(2)}) copy-start(s32[128,2]{0,1:T(2,128)} %get-tuple-element.15) | copy-start | bytes 3076
  123.5 41.3 %copy-start.6 = (f32[128,2]{0,1:T(2,128)S(1)}, f32[128,2]{0,1:T(2,128)}, u32[]{:S(2)}) copy-start(f32[128,2]{0,1:T(2,128)} %param.13) | copy-start | bytes 3076
  123.5 41.4 %copy-start.4 = (s32[128,2]{0,1:T(2,128)S(1)}, s32[128,2]{0,1:T(2,128)}, u32[]{:S(2)}) copy-start(s32[128,2]{0,1:T(2,128)} %copy-done.3) | copy-start | bytes 3076
  154.0 34.1 %all-to-all-start.3 = ((bf16[16,8,4096]{2,1,0:T(8,128)(2,1)}), bf16[16,8,4096]{2,1,0:T(8,128)(2,1)S(1)}, u32[]{:S(2)}, u32[]{:S(2)}) async-start(bf16[16,8,4096]{2,1,0:T(8,128)(2,1)} %fusion.5), calls=%async_computation.3 | async-start | bytes 2097152 | tf_op jit(solution)/shard_map/all_to_all | solution.py:15
  167.8 1.4 collective-permute-start.5

commit v6 on v5

--- a/solution.py
+++ b/solution.py
@@ -76,14 +76,13 @@
     large = cap * 2 // 3
     small = cap - large
 
-    flat = expert_ids.reshape(-1)
-    pairs = flat.shape[0]
-    onehot = flat[:, None] == jnp.arange(experts, dtype=jnp.int32)[None, :]
-    steps = jnp.arange(pairs, dtype=jnp.int32)
-    before = dot32((steps[:, None] > steps[None, :]).astype(BF), onehot.astype(BF))
-    rank = jnp.sum(jnp.where(onehot, before, 0.0), axis=1).astype(jnp.int32)
     ids = expert_ids[:, :, None]
-    rank = rank.reshape(tok_rows, top, 1)
+    named = ids == jnp.arange(experts, dtype=jnp.int32)[None, None, :]
+    steps = jnp.arange(tok_rows, dtype=jnp.int32)
+    counts = jnp.sum(named.astype(F32), axis=1).astype(BF)
+    before = dot32((steps[:, None] > steps[None, :]).astype(BF), counts)
+    rank = jnp.sum(jnp.where(named, before[:, None, :], 0.0), axis=2, keepdims=True).astype(jnp.int32)
+
     values = hidden_states.astype(F32)
     factor = lax.rsqrt(jnp.mean(values * values, axis=1, keepdims=True) + 1e-06)
     normed = (values * factor * norm_gain[None, :]).astype(BF)

time: 191 us -> 191 us (level)
  transfers between devices with their start and end apart: 10 -> 10, of which waited for: 5 -> 4; matrix products, arithmetic and copies ran while one was open for 31% -> 31% of each run, Pallas kernels for 0% -> 0%
where the time goes in v6:
time: 191 us; the launch traced here: 190 us
  waiting for transfers between devices  80.7 us (42%)
  matrix products  49.5 us (26%)
  starting transfers between devices  37 us (19%)
  other arithmetic  11.8 us (6%)
  local copies, waits for them, and re-layouts  9.54 us (5%)
    all_to_all x4, waiting for transfers between devices, all_to_all(): lax.all_to_all(x, 'node', split_axis=0, concat_axis=0, axis_index_groups=...  80.7 us
    dot_general x14, matrix products, dot32(): return jnp.dot(a, b, preferred_element_type=F32)  43.9 us
    all_to_all x4, starting transfers between devices, all_to_all(): lax.all_to_all(x, 'node', split_axis=0, concat_axis=0, axis_index_groups=...  35.7 us
    dot_general x2, matrix products, send(): lax.dot_general(placed, normed, (((0,), (0,)), ((), ())), preferred_eleme...  5.54 us
  transfers between devices with their start and end apart: 10, of which 4 were waited for; matrix products, arithmetic and copies ran while one was open for 31% of the time, Pallas kernels for 0%

profile of v6, /device:TPU:0, one launch (start us, length us, event | category | flops | bytes accessed | tf_op | source)
XLA Modules:
  0.0 190.1 jit_solution(10572402499302329739)
XLA Ops:
  0.6 1.5 fusion.28
  2.2 0.7 convert_reduce_fusion
  2.9 0.1 fusion.79
  3.0 0.7 select_reduce_fusion.2
  3.7 1.3 and_select_fusion.1
  5.0 0.1 fusion.57
  5.1 3.4 %convolution_convert_fusion = bf16[256,4096]{1,0:T(8,128)(2,1)} fusion(pred[128,256]{1,0:T(8,128)(4,1)S(1)} %fusion.57, bf16[128,4096]{1,0:T(8,128)(2,1)} %param.10, f32[4096]{0:T(1024)} %param.11, f32[128]{0:T(128)S(1)} %add_rsqrt_fusion), kind=kOutput, calls=%fused_computation.1 | convolution fusion | flops 271581184 | bytes 3195392 | tf_op jit(solution)/shard_map/dot_general | solution.py:104
  8.5 8.5 %all-to-all-start = ((bf16[16,16,4096]{2,1,0:T(8,128)(2,1)}), bf16[16,16,4096]{2,1,0:T(8,128)(2,1)S(1)}, u32[]{:S(2)}, u32[]{:S(2)}) async-start(bf16[16,16,4096]{2,1,0:T(8,128)(2,1)} %bitcast.111), calls=%async_computation | async-start | bytes 4194304 | tf_op jit(solution)/shard_map/all_to_all | solution.py:15
  16.9 0.1 collective-permute-start.3
  17.7 0.6 fusion.91
  18.3 0.5 collective-permute-start.1
  18.8 1.1 reshape.114
  19.9 0.6 broadcast_select_fusion.1
  20.6 0.1 collective-permute-start
  20.7 0.5 collective-permute-start.2
  21.2 0.1 collective-permute-start.4
  21.3 0.8 fusion.72
  22.0 2.2 %fusion.4 = bf16[16,8,4096]{2,1,0:T(8,128)(2,1)} fusion(pred[128,128]{1,0:T(8,128)(4,1)S(1)} %fusion.72, bf16[128,4096]{1,0:T(8,128)(2,1)S(1)} %copy-done, f32[4096]{0:T(1024)S(1)} %copy-done.3, f32[128]{0:T(128)} %copy-done.8), kind=kOutput, calls=%fused_computation.10 | convolution fusion | flops 136839168 | bytes 2130432 | tf_op jit(solution)/shard_map/dot_general | solution.py:104
  24.2 0.0 collective-permute-done.1
  24.2 0.7 convert.8
  25.0 0.1 pad_maximum_fusion
  25.1 0.1 copy.53
  25.2 0.1 convert_element_type.84
  25.3 0.0 collective-permute-done
  25.3 0.2 copy.52
  25.5 0.8 reshape.115
  26.3 2.3 %maximum_maximum_fusion = bf16[16,8,5248]{2,1,0:T(8,128)(2,1)} fusion(bf16[16,8,1024]{2,1,0:T(8,128)(2,1)} %reshape.115, bf16[16,8,4096]{2,1,0:T(8,128)(2,1)S(1)} %copy-done.2, bf16[5248]{0:T(1024)(128)(2,1)S(1)} %fusion.83), kind=kLoop, calls=%fused_computation.39 | loop fusion | flops 4030464 | bytes 2664704 | tf_op jit(solution)/shard_map/concatenate | solution.py:128
  28.5 31.5 %all-to-all-done = bf16[16,16,4096]{2,1,0:T(8,128)(2,1)S(1)} async-done(((bf16[16,16,4096]{2,1,0:T(8,128)(2,1)}), bf16[16,16,4096]{2,1,0:T(8,128)(2,1)S(1)}, u32[]{:S(2)}, u32[]{:S(2)}) %all-to-all-start) | async-done | bytes 2097184 | tf_op jit(solution)/shard_map/all_to_all | solution.py:15
  60.0 10.0 %all-to-all-start.1 = ((bf16[16,8,5248]{2,1,0:T(8,128)(2,1)}), bf16[16,8,5248]{2,1,0:T(8,128)(2,1)S(1)}, u32[]{:S(2)}, u32[]{:S(2)}) async-start(bf16[16,8,5248]{2,1,0:T(8,128)(2,1)} %maximum_maximum_fusion), calls=%async_computation.1 | async-start | bytes 2686976 | tf_op jit(solution)/shard_map/all_to_all | solution.py:15
  70.0 3.9 %fusion.24 = f32[256,384]{1,0:T(8,128)} fusion(bf16[256,4096]{1,0:T(8,128)(2,1)S(1)} %bitcast.104, bf16[1,4096,384]{2,1,0:T(8,128)(2,1)} %param.14), kind=kOutput, calls=%fused_computation.30 | convolution fusion | flops 805306368 | bytes 5636096 | tf_op jit(solution)/shard_map/dot_general | solution.py:11
  73.9 0.0 collective-permute-done.3
  73.9 3.9 %fusion.8 = f32[256,384]{1,0:T(8,128)} fusion(bf16[256,4096]{1,0:T(8,128)(2,1)S(1)} %bitcast.105, bf16[1,4096,384]{2,1,0:T(8,128)(2,1)} %collective-permute-done.3), kind=kOutput, calls=%fused_computation.14 | convolution fusion | flops 805306368 | bytes 5636096 | tf_op jit(solution)/shard_map/dot_general | solution.py:11
  77.8 7.4 %fusion.16 = f32[256,4096]{1,0:T(8,128)} fusion(bf16[1,384,4096]{2,1,0:T(8,128)(2,1)} %param.16, bf16[256,4096]{1,0:T(8,128)(2,1)S(1)} %bitcast.106, bf16[1,4096,384]{2,1,0:T(8,128)(2,1)} %param.15, f32[256,384]{1,0:T(8,128)} %fusion.24), kind=kOutput, calls=%fused_computation.22 | convolution fusion | flops 1611202560 | bytes 12976128 | tf_op jit(solution)/shard_map/dot_general | solution.py:11
  85.1 0.0 collective-permute-done.2
  85.1 0.0 collective-permute-done.4
  85.1 8.0 %fusion = bf16[256,4096]{1,0:T(8,128)(2,1)} fusion(f32[256,4096]{1,0:T(8,128)} %fusion.16, bf16[1,384,4096]{2,1,0:T(8,128)(2,1)} %collective-permute-done.4, f32[256,384]{1,0:T(8,128)} %fusion.8, bf16[256,4096]{1,0:T(8,128)(2,1)S(1)} %bitcast.107, bf16[1,4096,384]{2,1,0:T(8,128)(2,1)} %collective-permute-done.2), kind=kOutput, calls=%fused_computation.2 | convolution fusion | flops 1613299712 | bytes 15073280 | tf_op jit(solution)/shard_map/dot_general | solution.py:11
  93.1 3.2 %pad.9 = bf16[16,16,4608]{2,1,0:T(8,128)(2,1)} pad(bf16[16,16,4096]{2,1,0:T(8,128)(2,1)} %bitcast.110, bf16[]{:T(256)} %constant.48.clone.1), padding=0_0x0_0x0_512 | pad | bytes 4456450 | tf_op jit(solution)/shard_map/jit(_pad)/pad | solution.py:133
  96.3 3.0 %all-to-all-done.1 = bf16[16,8,5248]{2,1,0:T(8,128)(2,1)S(1)} async-done(((bf16[16,8,5248]{2,1,0:T(8,128)(2,1)}), bf16[16,8,5248]{2,1,0:T(8,128)(2,1)S(1)}, u32[]{:S(2)}, u32[]{:S(2)}) %all-to-all-start.1) | async-done | bytes 1343520 | tf_op jit(solution)/shard_map/all_to_all | solution.py:15
  99.4 0.1 reshape.129
  99.5 0.2 fusion.70
  99.7 0.1 reshape.123
  99.8 0.2 convolution_convert_fusion.2
  100.0 0.8 constant_dynamic-update-slice_fusion
  100.8 6.5 %all-to-all-start.2 = ((bf16[16,16,4608]{2,1,0:T(8,128)(2,1)}), bf16[16,16,4608]{2,1,0:T(8,128)(2,1)}, u32[]{:S(2)}, u32[]{:S(2)}) async-start(bf16[16,16,4608]{2,1,0:T(8,128)(2,1)} %constant_dynamic-update-slice_fusion), calls=%async_computation.2 | async-start | bytes 4718592 | tf_op jit(solution)/shard_map/all_to_all | solution.py:15
  107.3 3.3 %fusion.26 = f32[128,384]{1,0:T(8,128)} fusion(bf16[1,4096,384]{2,1,0:T(8,128)(2,1)} %param.14, bf16[16,8,5248]{2,1,0:T(8,128)(2,1)S(1)} %all-to-all-done.1), kind=kOutput, calls=%fused_computation.32 | convolution fusion | flops 402653184 | bytes 4390912 | tf_op jit(solution)/shard_map/dot_general | solution.py:11
  110.6 3.3 %fusion.10 = f32[128,384]{1,0:T(8,128)} fusion(bf16[1,4096,384]{2,1,0:T(8,128)(2,1)} %collective-permute-done.3, bf16[16,8,5248]{2,1,0:T(8,128)(2,1)S(1)} %all-to-all-done.1), kind=kOutput, calls=%fused_computation.16 | convolution fusion | flops 402653184 | bytes 4390912 | tf_op jit(solution)/shard_map/dot_general | solution.py:11
  113.9 4.4 %fusion.18 = f32[128,4096]{1,0:T(8,128)S(1)} fusion(bf16[1,384,4096]{2,1,0:T(8,128)(2,1)} %param.16, bf16[1,4096,384]{2,1,0:T(8,128)(2,1)} %param.15, bf16[16,8,5248]{2,1,0:T(8,128)(2,1)S(1)} %all-to-all-done.1, f32[128,384]{1,0:T(8,128)} %fusion.26), kind=kOutput, calls=%fused_computation.24 | convolution fusion | flops 805601280 | bytes 9633792 | tf_op jit(solution)/shard_map/dot_general | solution.py:11
  118.3 5.4 %fusion.5 = bf16[16,8,4096]{2,1,0:T(8,128)(2,1)} fusion(f32[128,4096]{1,0:T(8,128)S(1)} %fusion.18, bf16[1,384,4096]{2,1,0:T(8,128)(2,1)} %collective-permute-done.4, f32[128,384]{1,0:T(8,128)} %fusion.10, bf16[1,4096,384]{2,1,0:T(8,128)(2,1)} %collective-permute-done.2, bf16[16,8,5248]{2,1,0:T(8,128)(2,1)S(1)} %all-to-all-done.1), kind=kOutput, calls=%fused_computation.11 | convolution fusion | flops 806649856 | bytes 10682368 | tf_op jit(solution)/shard_map/dot_general | solution.py:11
  123.6 30.4 %all-to-all-done.2 = bf16[16,16,4608]{2,1,0:T(8,128)(2,1)} async-done(((bf16[16,16,4608]{2,1,0:T(8,128)(2,1)}), bf16[16,16,4608]{2,1,0:T(8,128)(2,1)}, u32[]{:S(2)}, u32[]{:S(2)}) %all-to-all-start.2) | async-done | bytes 2359328 | tf_op jit(solution)/shard_map/all_to_all | solution.py:15
  154.0 10.8 %all-to-all-start.3 = ((bf16[16,8,4096]{2,1,0:T(8,128)(2,1)}), bf16[16,8,4096]{2,1,0:T(8,128)(2,1)S(1)}, u32[]{:S(2)}, u32[]{:S(2)}) async-start(bf16[16,8,4096]{2,1,0:T(8,128)(2,1)} %fusion.5), calls=%async_computation.3 | async-start | bytes 2097152 | tf_op jit(solution)/shard_map/all_to_all | solution.py:15
  164.9 0.1 select_reduce_fusion.1
  165.0 0.1 select_reduce_fusion
  165.1 1.8 slice.56
  167.0 1.0 broadcast_select_fusion.2
  167.9 0.1 collective-permute-start.5
  168.0 0.4 fusion.81
  168.5 1.8 convolution_add_fusion.2
  170.3 0.0 collective-permute-done.5
  170.3 1.0 select_bitcast_fusion.1
  171.3 0.3 copy.54
  171.6 0.9 reshape.127
  172.5 15.7 %all-to-all-done.3 = bf16[16,8,4096]{2,1,0:T(8,128)(2,1)S(1)} async-done(((bf16[16,8,4096]{2,1,0:T(8,128)(2,1)}), bf16[16,8,4096]{2,1,0:T(8,128)(2,1)S(1)}, u32[]{:S(2)}, u32[]{:S(2)}) %all-to-all-start.3) | async-done | bytes 1048608 | tf_op jit(solution)/shard_map/all_to_all | solution.py:15
  188.2 0.4 fusion.48
  188.6 1.5 fusion.3
  (33 shorter events, 0.2 us)
Async XLA Ops:
  2.2 6.3 %copy-start.8 = (f32[128]{0:T(128)}, f32[128]{0:T(128)S(1)}, u32[]{:S(2)}) copy-start(f32[128]{0:T(128)S(1)} %add_rsqrt_fusion) | copy-start | bytes 1540
  5.0 3.5 %copy-start.4 = (s32[128,2]{0,1:T(2,128)}, s32[128,2]{0,1:T(2,128)S(1)}, u32[]{:S(2)}) copy-start(s32[128,2]{0,1:T(2,128)S(1)} %get-tuple-element.14) | copy-start | bytes 3076
  8.5 9.2 %copy-start.9 = (s32[8,2]{0,1:T(2,128)S(1)}, s32[8,2]{0,1:T(2,128)}, u32[]{:S(2)}) copy-start(s32[8,2]{0,1:T(2,128)} %param.18) | copy-start | bytes 196
  8.5 13.6 %copy-start = (bf16[128,4096]{1,0:T(8,128)(2,1)S(1)}, bf16[128,4096]{1,0:T(8,128)(2,1)}, u32[]{:S(2)}) copy-start(bf16[128,4096]{1,0:T(8,128)(2,1)} %param.10) | copy-start | bytes 3145732
  8.5 13.6 %copy-start.3 = (f32[4096]{0:T(1024)S(1)}, f32[4096]{0:T(1024)}, u32[]{:S(2)}) copy-start(f32[4096]{0:T(1024)} %param.11) | copy-start | bytes 49156
  8.5 51.5 %all-to-all-start = ((bf16[16,16,4096]{2,1,0:T(8,128)(2,1)}), bf16[16,16,4096]{2,1,0:T(8,128)(2,1)S(1)}, u32[]{:S(2)}, u32[]{:S(2)}) async-start(bf16[16,16,4096]{2,1,0:T(8,128)(2,1)} %bitcast.111), calls=%async_computation | async-start | bytes 4194304 | tf_op jit(solution)/shard_map/all_to_all | solution.py:15
  16.9 56.9 %collective-permute-start.3 = (bf16[1,4096,384]{2,1,0:T(8,128)(2,1)}, bf16[1,4096,384]{2,1,0:T(8,128)(2,1)}, u32[]{:S(2)}, u32[]{:S(2)}) collective-permute-start(bf16[1,4096,384]{2,1,0:T(8,128)(2,1)} %param.15), channel_id=1, source_target_pairs={{0,1},{1,0},{2,3},{3,2},{4,5},{5,4},{6,7},{7,6},{8,9},{9,8},{10,11... | collective-permute-start | bytes 9437192 | tf_op jit(solution)/shard_map/ppermute | solution.py:93
  18.3 5.9 %collective-permute-start.1 = (s32[8,2]{0,1:T(2,128)}, s32[8,2]{0,1:T(2,128)}, u32[]{:S(2)}, u32[]{:S(2)}) collective-permute-start(s32[8,2]{0,1:T(2,128)} %get-tuple-element.17), channel_id=1, source_target_pairs={{0,1},{1,0},{2,3},{3,2},{4,5},{5,4},{6,7},{7,6},{8,9},{9,8},{10,11... | collective-permute-start | bytes 200 | tf_op jit(solution)/shard_map/ppermute | solution.py:29
  19.9 5.1 %copy-start.10 = (bf16[8,2]{0,1:T(2,128)(2,1)S(1)}, bf16[8,2]{0,1:T(2,128)(2,1)}, u32[]{:S(2)}) copy-start(bf16[8,2]{0,1:T(2,128)(2,1)} %get-tuple-element.16) | copy-start | bytes 100
  20.6 4.7 %collective-permute-start = (bf16[8,16,512]{2,1,0:T(8,128)(2,1)S(1)}, bf16[8,16,512]{2,1,0:T(8,128)(2,1)S(1)}, u32[]{:S(2)}, u32[]{:S(2)}) collective-permute-start(bf16[8,16,512]{2,1,0:T(8,128)(2,1)S(1)} %bitcast.114), channel_id=1, source_target_pairs={{0,1},{1,0},{2,3},{3,2},{4,5},{5,4},{6,7},{7,6},{8,9},{9,8},{10,11... | collective-permute-start | bytes 393224 | tf_op jit(solution)/shard_map/ppermute | solution.py:32
  20.7 64.5 %collective-permute-start.2 = (bf16[1,4096,384]{2,1,0:T(8,128)(2,1)}, bf16[1,4096,384]{2,1,0:T(8,128)(2,1)}, u32[]{:S(2)}, u32[]{:S(2)}) collective-permute-start(bf16[1,4096,384]{2,1,0:T(8,128)(2,1)} %param.14), channel_id=1, source_target_pairs={{0,1},{1,0},{2,3},{3,2},{4,5},{5,4},{6,7},{7,6},{8,9},{9,8},{10,11... | collective-permute-start | bytes 9437192 | tf_op jit(solution)/shard_map/ppermute | solution.py:93
  21.2 64.0 %collective-permute-start.4 = (bf16[1,384,4096]{2,1,0:T(8,128)(2,1)}, bf16[1,384,4096]{2,1,0:T(8,128)(2,1)}, u32[]{:S(2)}, u32[]{:S(2)}) collective-permute-start(bf16[1,384,4096]{2,1,0:T(8,128)(2,1)} %param.16), channel_id=1, source_target_pairs={{0,1},{1,0},{2,3},{3,2},{4,5},{5,4},{6,7},{7,6},{8,9},{9,8},{10,11... | collective-permute-start | bytes 9437192 | tf_op jit(solution)/shard_map/ppermute | solution.py:93
  24.2 2.1 %copy-start.2 = (bf16[16,8,4096]{2,1,0:T(8,128)(2,1)S(1)}, bf16[16,8,4096]{2,1,0:T(8,128)(2,1)}, u32[]{:S(2)}) copy-start(bf16[16,8,4096]{2,1,0:T(8,128)(2,1)} %fusion.4) | copy-start | bytes 3145732
  60.0 39.3 %all-to-all-start.1 = ((bf16[16,8,5248]{2,1,0:T(8,128)(2,1)}), bf16[16,8,5248]{2,1,0:T(8,128)(2,1)S(1)}, u32[]{:S(2)}, u32[]{:S(2)}) async-start(bf16[16,8,5248]{2,1,0:T(8,128)(2,1)} %maximum_maximum_fusion), calls=%async_computation.1 | async-start | bytes 2686976 | tf_op jit(solution)/shard_map/all_to_all | solution.py:15
  100.8 53.2 %all-to-all-start.2 = ((bf16[16,16,4608]{2,1,0:T(8,128)(2,1)}), bf16[16,16,4608]{2,1,0:T(8,128)(2,1)}, u32[]{:S(2)}, u32[]{:S(2)}) async-start(bf16[16,16,4608]{2,1,0:T(8,128)(2,1)} %constant_dynamic-update-slice_fusion), calls=%async_computation.2 | async-start | bytes 4718592 | tf_op jit(solution)/shard_map/all_to_all | solution.py:15
  123.6 41.2 %copy-start.6 = (s32[128,2]{0,1:T(2,128)S(1)}, s32[128,2]{0,1:T(2,128)}, u32[]{:S(2)}) copy-start(s32[128,2]{0,1:T(2,128)} %get-tuple-element.15) | copy-start | bytes 3076
  123.6 41.2 %copy-start.7 = (f32[128,2]{0,1:T(2,128)S(1)}, f32[128,2]{0,1:T(2,128)}, u32[]{:S(2)}) copy-start(f32[128,2]{0,1:T(2,128)} %param.13) | copy-start | bytes 3076
  123.6 41.4 %copy-start.5 = (s32[128,2]{0,1:T(2,128)S(1)}, s32[128,2]{0,1:T(2,128)}, u32[]{:S(2)}) copy-start(s32[128,2]{0,1:T(2,128)} %copy-done.4) | copy-start | bytes 3076
  154.0 34.2 %all-to-all-start.3 = ((bf16[16,8,4096]{2,1,0:T(8,128)(2,1)}), bf16[16,8,4096]{2,1,0:T(8,128)(2,1)S(1)}, u32[]{:S(2)}, u32[]{:S(2)}) async-start(bf16[16,8,4096]{2,1,0:T(8,128)(2,1)} %fusion.5), calls=%async_computation.3 | async-start | bytes 2097152 | tf_op jit(solution)/shard_map/all_to_all | solution.py:15
  167.9 2.3 %collective-permute-start.5 = (bf16[16,8,512]{2,1,0:T(8,128)(2,1)S(1)}, bf16[16,8,512]{2,1,0:T(8,128)(2,1)S(1)}, u32[]{:S(2)}, u32[]{:S(2)}) collective-permute-start(bf16[16,8,512]{2,1,0:T(8,128)(2,1)S(1)} %broadcast_select_fusion.2), channel_id=1, source_target_pairs={{0,1},{1,0},{2,3},{3,2},{4,5},{5,4},{6,7},{7,6},{8,9},{9,8},{10,11... | collective-permute-start | bytes 393224 | tf_op jit(solution)/shard_map/ppermute | solution.py:51
  171.3 17.3 %copy-start.1 = (f32[128,4096]{1,0:T(8,128)S(1)}, f32[128,4096]{1,0:T(8,128)}, u32[]{:S(2)}) copy-start(f32[128,4096]{1,0:T(8,128)} %convolution_add_fusion.2) | copy-start | bytes 6291460
